TPU v7x, 512 devices: a whole 4x4x16 slice. The times are simulated.
512 devices in a mesh: dp: 32 (over x, y, core), seq: 16 (over z).
Axes of the slice: x: 4, y: 4, z: 16, core: 2. Of those that a mesh axis runs over, the one named last changes fastest.
Arguments:
- query_rows: bfloat16 [64, 1024, 2048], P('dp', 'seq'), may hold values from -6.5 to 6.5
- key_rows: bfloat16 [64, 1024, 2048], P('dp', 'seq'), may hold values from -6.5 to 6.5
- value_rows: bfloat16 [64, 1024, 2048], P('dp', 'seq'), may hold values from -6 to 6
- cotangent: bfloat16 [64, 1024, 2048], P('dp', 'seq'), may hold values from -6 to 6
- segment_ids: int32 [64, 1024], P('dp', 'seq'), may hold values from 0 to 15, as said below
- moved_slot: int32 [32], P('dp'), may hold values from 0 to 2, as said below
- query_gain: float32 [32, 64], P('seq'), may hold values from 0.5 to 5.6
- key_gain: float32 [32, 64], P('seq'), may hold values from 0.5 to 5.6
Outputs:
- attended: bfloat16 [64, 1024, 2048], P('dp', 'seq')
- grad_queries: bfloat16 [64, 1024, 2048], P('dp', 'seq')
- grad_keys: bfloat16 [64, 1024, 2048], P('dp', 'seq')
- grad_values: bfloat16 [64, 1024, 2048], P('dp', 'seq')
- grad_query_gain: float32 [32, 64], P('seq', 'dp')
- grad_key_gain: float32 [32, 64], P('seq', 'dp')
Inputs may be any that keep to these rules, and one draw needn't show every extreme that they name: `segment_ids`: within a pack the ids start at 0 and never fall; every image spans a whole multiple of 64 patches on a multiple of 64; some pack is a single image of 1024 patches. `moved_slot`: group g and group g xor 16 hold the same value; the value 2 means that no pack is traded, any other value s that the packs in slot s of the two groups trade places.
All inputs are finite; a program needn't handle non-finite values.
Results may differ from a plain program's by a relative error of at most 0.011.
The roundings to bfloat16 on the way count: a program that leaves them out, or rounds other values in their place, can miss the bound.
Values may be sent and summed in bfloat16 or wider, within the bound.
A program may use at most 64 MiB of HBM per device.

v0:
```python
from functools import partial

import jax
import jax.numpy as jnp
from jax import lax
from jax.sharding import PartitionSpec as P

HEAD_DIM = 64


EPSILON = 1e-06


def from_partner(value, axis, distance):
    mask = 2**distance
    pairs = [(source, source ^ mask) for source in range(lax.axis_size(axis))]
    return lax.ppermute(value, axis, pairs)


def as_sent(x):

    def short(part):
        return part.astype(jnp.bfloat16) if part.dtype == jnp.float32 else part

    return jax.tree.map(short, x)


def normalize(raw, gain):
    average = jnp.mean(raw, axis=-1, keepdims=True)
    centred = raw - average
    inv_std = lax.rsqrt(jnp.mean(centred * centred, axis=-1, keepdims=True) + EPSILON)
    unit_rows = centred * inv_std
    return (unit_rows, inv_std, (unit_rows * gain).astype(jnp.bfloat16))


def norm_back(grad, unit_rows, inv_std, gain):
    scaled = grad * gain
    inner = (
        scaled
        - jnp.mean(scaled, axis=-1, keepdims=True)
        - unit_rows * jnp.mean(scaled * unit_rows, axis=-1, keepdims=True)
    )
    return ((inv_std * inner).astype(jnp.bfloat16), jnp.sum(grad * unit_rows, axis=0))


def pack_work(query_gain, key_gain, pieces):
    query_part, key_part, value_part, cot_part, seg_part = pieces
    length = query_part.shape[0]
    head_count = query_part.shape[1] // HEAD_DIM
    row_shape = (length, head_count, HEAD_DIM)
    score_scale = HEAD_DIM ** (-0.5)
    query_unit, query_scale, query_norm = normalize(
        query_part.astype(jnp.float32).reshape(row_shape), query_gain
    )
    key_unit, key_scale, key_norm = normalize(
        key_part.astype(jnp.float32).reshape(row_shape), key_gain
    )
    value_heads = value_part.reshape(row_shape)
    cot_heads = cot_part.reshape(row_shape)
    block_rows = min(512, length)
    key_acc = jnp.zeros(row_shape, jnp.float32)
    value_acc = jnp.zeros(row_shape, jnp.float32)
    attended_parts = []
    query_parts = []
    for row_start in range(0, length, block_rows):
        query_block = query_norm[row_start : row_start + block_rows]
        cot_block = cot_heads[row_start : row_start + block_rows]
        seg_block = seg_part[row_start : row_start + block_rows]
        scores = (
            jnp.einsum("qhd,khd->hqk", query_block, key_norm, preferred_element_type=jnp.float32)
            * score_scale
        )
        same = seg_block[:, None] == seg_part[None, :]
        scores = jnp.where(same[None], scores, -jnp.inf)
        row_max = jnp.max(scores, axis=-1, keepdims=True)
        exponent = jnp.exp(scores - row_max)
        weights = exponent / jnp.sum(exponent, axis=-1, keepdims=True)
        weights_low = weights.astype(jnp.bfloat16)
        attended_full = jnp.einsum(
            "hqk,khd->qhd", weights_low, value_heads, preferred_element_type=jnp.float32
        )
        row_delta = jnp.sum(cot_block.astype(jnp.float32) * attended_full, axis=-1)
        prob_grad = jnp.einsum(
            "qhd,khd->hqk", cot_block, value_heads, preferred_element_type=jnp.float32
        )
        score_grad = (weights * (prob_grad - jnp.transpose(row_delta)[:, :, None])).astype(
            jnp.bfloat16
        )
        value_acc = value_acc + jnp.einsum(
            "hqk,qhd->khd", weights_low, cot_block, preferred_element_type=jnp.float32
        )
        key_acc = (
            key_acc
            + jnp.einsum(
                "hqk,qhd->khd", score_grad, query_block, preferred_element_type=jnp.float32
            )
            * score_scale
        )
        query_parts.append(
            jnp.einsum("hqk,khd->qhd", score_grad, key_norm, preferred_element_type=jnp.float32)
            * score_scale
        )
        attended_parts.append(attended_full.astype(jnp.bfloat16))
    attended = jnp.concatenate(attended_parts, axis=0)
    norm_query_grad = jnp.concatenate(query_parts, axis=0)
    grad_queries, gain_query = norm_back(norm_query_grad, query_unit, query_scale, query_gain)
    grad_keys, gain_key = norm_back(key_acc, key_unit, key_scale, key_gain)
    flat = (length, head_count * HEAD_DIM)
    return (
        attended.reshape(flat),
        grad_queries.reshape(flat),
        grad_keys.reshape(flat),
        value_acc.astype(jnp.bfloat16).reshape(flat),
        gain_query,
        gain_key,
    )


def attend_packs(query_heads, key_heads, value_heads, cot_heads, seg_heads, query_gain, key_gain):
    return lax.map(
        partial(pack_work, query_gain, key_gain),
        (query_heads, key_heads, value_heads, cot_heads, seg_heads),
    )


def body(
    query_rows, key_rows, value_rows, cotangent, segment_ids, moved_slot, query_gain, key_gain
):
    pack_count = query_rows.shape[0]
    pair_bit = lax.axis_size("dp").bit_length() - 2
    moved_here = moved_slot[0]
    use_remote = jnp.arange(pack_count) == moved_here
    remote = from_partner(
        (query_rows, key_rows, value_rows, cotangent, segment_ids), "dp", pair_bit
    )
    wide_mask = use_remote[:, None, None]
    query_rows = jnp.where(wide_mask, remote[0], query_rows)
    key_rows = jnp.where(wide_mask, remote[1], key_rows)
    value_rows = jnp.where(wide_mask, remote[2], value_rows)
    cotangent = jnp.where(wide_mask, remote[3], cotangent)
    segment_ids = jnp.where(use_remote[:, None], remote[4], segment_ids)
    seg_spread = jnp.broadcast_to(
        segment_ids[:, :, None], segment_ids.shape + (lax.axis_size("seq"),)
    )
    heads_view = (
        lax.all_to_all(query_rows, "seq", split_axis=2, concat_axis=1, tiled=True),
        lax.all_to_all(key_rows, "seq", split_axis=2, concat_axis=1, tiled=True),
        lax.all_to_all(value_rows, "seq", split_axis=2, concat_axis=1, tiled=True),
        lax.all_to_all(cotangent, "seq", split_axis=2, concat_axis=1, tiled=True),
        lax.all_to_all(seg_spread, "seq", split_axis=2, concat_axis=1, tiled=True),
    )
    results = attend_packs(
        heads_view[0],
        heads_view[1],
        heads_view[2],
        heads_view[3],
        heads_view[4][..., 0],
        query_gain,
        key_gain,
    )
    back_rows = (
        lax.all_to_all(as_sent(results[0]), "seq", split_axis=1, concat_axis=2, tiled=True),
        lax.all_to_all(results[1], "seq", split_axis=1, concat_axis=2, tiled=True),
        lax.all_to_all(results[2], "seq", split_axis=1, concat_axis=2, tiled=True),
        lax.all_to_all(results[3], "seq", split_axis=1, concat_axis=2, tiled=True),
    )
    attended, grad_queries, grad_keys, grad_values = back_rows
    gain_query, gain_key = (results[4], results[5])
    grad_query_gain, grad_key_gain = (
        lax.psum_scatter(jnp.sum(gain_query, axis=0), "dp", scatter_dimension=1, tiled=True),
        lax.psum_scatter(jnp.sum(gain_key, axis=0), "dp", scatter_dimension=1, tiled=True),
    )
    return (attended, grad_queries, grad_keys, grad_values, grad_query_gain, grad_key_gain)


def solution(mesh):
    return jax.shard_map(
        body,
        mesh=mesh,
        in_specs=(
            P("dp", "seq", None),
            P("dp", "seq", None),
            P("dp", "seq", None),
            P("dp", "seq", None),
            P("dp", "seq"),
            P("dp"),
            P("seq", None),
            P("seq", None),
        ),
        out_specs=(
            P("dp", "seq", None),
            P("dp", "seq", None),
            P("dp", "seq", None),
            P("dp", "seq", None),
            P("seq", "dp"),
            P("seq", "dp"),
        ),
        check_vma=False,
    )
```

profile of v0, /device:TPU:1, one launch (start us, length us, event | category | flops | bytes accessed | tf_op | source)
XLA Modules:
  0.0 469.8 jit_solution(17874097258829290109)
XLA Ops:
  0.6 5.5 %collective-permute-start.1 = (s32[2,64]{1,0:T(2,128)}, s32[2,64]{1,0:T(2,128)S(1)}, u32[]{:S(2)}, u32[]{:S(2)}) collective-permute-start(s32[2,64]{1,0:T(2,128)} %param.14), channel_id=1, source_target_pairs={{0,256},{16,272},{32,288},{48,304},{64,320},{80,336},{96,352},{112... | collective-permute-start | bytes 1544 | tf_op jit(solution)/shard_map/ppermute | solution.py:17
  6.1 1.9 collective-permute-start.2
  8.1 4.9 %collective-permute-start.3 = (bf16[2,64,2048]{2,1,0:T(8,128)(2,1)}, bf16[2,64,2048]{2,1,0:T(8,128)(2,1)S(1)}, u32[]{:S(2)}, u32[]{:S(2)}) collective-permute-start(bf16[2,64,2048]{2,1,0:T(8,128)(2,1)} %param.11), channel_id=1, source_target_pairs={{0,256},{16,272},{32,288},{48,304},{64,320},{80,336},{96,352},{112... | collective-permute-start | bytes 1572872 | tf_op jit(solution)/shard_map/ppermute | solution.py:17
  12.9 1.9 collective-permute-start
  14.9 4.9 %collective-permute-start.4 = (bf16[2,64,2048]{2,1,0:T(8,128)(2,1)}, bf16[2,64,2048]{2,1,0:T(8,128)(2,1)}, u32[]{:S(2)}, u32[]{:S(2)}) collective-permute-start(bf16[2,64,2048]{2,1,0:T(8,128)(2,1)} %param.13), channel_id=1, source_target_pairs={{0,256},{16,272},{32,288},{48,304},{64,320},{80,336},{96,352},{112... | collective-permute-start | bytes 1572872 | tf_op jit(solution)/shard_map/ppermute | solution.py:17
  21.9 14.9 %all-to-all-start.1 = ((s32[16,1,128]{2,1,0:T(1,128)}), s32[16,1,128]{2,1,0:T(1,128)S(1)}, u32[]{:S(2)}, u32[]{:S(2)}) async-start(s32[16,1,128]{2,1,0:T(1,128)} %reshape.278), calls=%async_computation.1 | async-start | bytes 16384 | tf_op jit(solution)/shard_map/all_to_all | solution.py:150
  36.8 5.5 %collective-permute-done = bf16[2,64,2048]{2,1,0:T(8,128)(2,1)S(1)} collective-permute-done((bf16[2,64,2048]{2,1,0:T(8,128)(2,1)}, bf16[2,64,2048]{2,1,0:T(8,128)(2,1)S(1)}, u32[]{:S(2)}, u32[]{:S(2)}) %collective-permute-start) | collective-permute-done | bytes 524320 | tf_op jit(solution)/shard_map/ppermute | solution.py:17
  43.1 10.5 %collective-permute-done.4 = bf16[2,64,2048]{2,1,0:T(8,128)(2,1)} collective-permute-done((bf16[2,64,2048]{2,1,0:T(8,128)(2,1)}, bf16[2,64,2048]{2,1,0:T(8,128)(2,1)}, u32[]{:S(2)}, u32[]{:S(2)}) %collective-permute-start.4) | collective-permute-done | bytes 524320 | tf_op jit(solution)/shard_map/ppermute | solution.py:17
  53.7 2.1 broadcast_select_fusion
  56.5 1.5 reshape.284
  58.1 17.3 %all-to-all-start.4 = ((bf16[16,2,8192]{2,1,0:T(2,128)(2,1)}), bf16[16,2,8192]{2,1,0:T(2,128)(2,1)S(1)}, u32[]{:S(2)}, u32[]{:S(2)}) async-start(bf16[16,2,8192]{2,1,0:T(2,128)(2,1)} %reshape.284), calls=%async_computation.4 | async-start | bytes 1048576 | tf_op jit(solution)/shard_map/all_to_all | solution.py:149
  76.1 1.5 reshape.280
  77.6 19.8 %all-to-all-done.4 = bf16[16,2,8192]{2,1,0:T(2,128)(2,1)S(1)} async-done(((bf16[16,2,8192]{2,1,0:T(2,128)(2,1)}), bf16[16,2,8192]{2,1,0:T(2,128)(2,1)S(1)}, u32[]{:S(2)}, u32[]{:S(2)}) %all-to-all-start.4) | async-done | bytes 524320 | tf_op jit(solution)/shard_map/all_to_all | solution.py:149
  97.4 12.9 %all-to-all-start.2 = ((bf16[16,2,8192]{2,1,0:T(2,128)(2,1)}), bf16[16,2,8192]{2,1,0:T(2,128)(2,1)S(1)}, u32[]{:S(2)}, u32[]{:S(2)}) async-start(bf16[16,2,8192]{2,1,0:T(2,128)(2,1)} %reshape.280), calls=%async_computation.2 | async-start | bytes 1048576 | tf_op jit(solution)/shard_map/all_to_all | solution.py:146
  111.1 1.5 reshape.282
  112.6 20.5 %all-to-all-done.2 = bf16[16,2,8192]{2,1,0:T(2,128)(2,1)S(1)} async-done(((bf16[16,2,8192]{2,1,0:T(2,128)(2,1)}), bf16[16,2,8192]{2,1,0:T(2,128)(2,1)S(1)}, u32[]{:S(2)}, u32[]{:S(2)}) %all-to-all-start.2) | async-done | bytes 524320 | tf_op jit(solution)/shard_map/all_to_all | solution.py:146
  133.1 12.2 %all-to-all-start.3 = ((bf16[16,2,8192]{2,1,0:T(2,128)(2,1)}), bf16[16,2,8192]{2,1,0:T(2,128)(2,1)S(1)}, u32[]{:S(2)}, u32[]{:S(2)}) async-start(bf16[16,2,8192]{2,1,0:T(2,128)(2,1)} %reshape.282), calls=%async_computation.3 | async-start | bytes 1048576 | tf_op jit(solution)/shard_map/all_to_all | solution.py:147
  146.0 1.5 reshape.276
  147.6 20.5 %all-to-all-done.3 = bf16[16,2,8192]{2,1,0:T(2,128)(2,1)S(1)} async-done(((bf16[16,2,8192]{2,1,0:T(2,128)(2,1)}), bf16[16,2,8192]{2,1,0:T(2,128)(2,1)S(1)}, u32[]{:S(2)}, u32[]{:S(2)}) %all-to-all-start.3) | async-done | bytes 524320 | tf_op jit(solution)/shard_map/all_to_all | solution.py:147
  168.1 12.2 %all-to-all-start = ((bf16[16,2,8192]{2,1,0:T(2,128)(2,1)}), bf16[16,2,8192]{2,1,0:T(2,128)(2,1)S(1)}, u32[]{:S(2)}, u32[]{:S(2)}) async-start(bf16[16,2,8192]{2,1,0:T(2,128)(2,1)} %reshape.276), calls=%async_computation | async-start | bytes 1048576 | tf_op jit(solution)/shard_map/all_to_all | solution.py:148
  182.9 1.8 copy.147
  185.4 1.8 copy.143
  187.9 1.8 copy.145
  189.8 13.3 %all-to-all-done = bf16[16,2,8192]{2,1,0:T(2,128)(2,1)S(1)} async-done(((bf16[16,2,8192]{2,1,0:T(2,128)(2,1)}), bf16[16,2,8192]{2,1,0:T(2,128)(2,1)S(1)}, u32[]{:S(2)}, u32[]{:S(2)}) %all-to-all-start) | async-done | bytes 524320 | tf_op jit(solution)/shard_map/all_to_all | solution.py:148
  203.7 1.8 copy.141
  205.6 74.3 %while.21 = (s32[]{:T(128)}, bf16[2,1024,128]{1,2,0:T(8,128)(2,1)}, bf16[2,1024,128]{1,2,0:T(8,128)(2,1)}, bf16[2,1024,128]{1,2,0:T(8,128)(2,1)}, bf16[2,1024,12...) while((s32[]{:T(128)}, bf16[2,1024,128]{1,2,0:T(8,128)(2,1)}, ...), condition=%wide.wide.region_17.18_spmd, body=%wide.wide.region_0.17_spmd.sunk | while | flops 1643777920 | bytes 133634168 | solution.py:120
  214.1 4.2 fusion.191
  218.3 2.9 fusion.192
  221.2 1.4 multiply_reduce_fusion.14
  224.8 1.4 convolution_multiply_fusion.6
  226.2 5.3 %fusion.193 = (f32[2,512]{1,0:T(2,128)}, f32[2,512,1024]{2,1,0:T(8,128)}) fusion(pred[512,1024]{1,0:T(8,128)(4,1)} %get-tuple-element.444, bf16[1024,2,64]{0,2,1:T(8,128)(2,1)} %copy-done.8, bf16[1024,2,64]{0,2,1:T(8,128)(2,1)S(1)} %bitcast.273, f32[2,64]{1,0:T(2,128)} %get-tuple-element.561, f32[1024,2]{0,1:T(2,128)S(1)} %add_rsqrt_fusion.7, ...), kind=kOutput, calls=%fused_computation.112.clone.clone.1 | convolution fusion | flops 139068416 | bytes 5133312 | tf_op jit(solution)/shard_map/while/body/eval_jaxpr/sub | solution.py:76
  231.6 2.8 fusion.194
  251.1 4.2 fusion.191
  255.3 2.9 fusion.192
  258.2 1.4 multiply_reduce_fusion.14
  261.9 1.4 convolution_multiply_fusion.6
  263.3 5.3 %fusion.193 = (f32[2,512]{1,0:T(2,128)}, f32[2,512,1024]{2,1,0:T(8,128)}) fusion(pred[512,1024]{1,0:T(8,128)(4,1)} %get-tuple-element.444, bf16[1024,2,64]{0,2,1:T(8,128)(2,1)} %copy-done.8, bf16[1024,2,64]{0,2,1:T(8,128)(2,1)S(1)} %bitcast.273, f32[2,64]{1,0:T(2,128)} %get-tuple-element.561, f32[1024,2]{0,1:T(2,128)S(1)} %add_rsqrt_fusion.7, ...), kind=kOutput, calls=%fused_computation.112.clone.clone.1 | convolution fusion | flops 139068416 | bytes 5133312 | tf_op jit(solution)/shard_map/while/body/eval_jaxpr/sub | solution.py:76
  268.6 2.8 fusion.194
  280.0 2.1 copy.128
  282.0 12.2 %all-to-all-start.5 = ((bf16[2,1024,128]{2,0,1:T(2,128)(2,1)}), bf16[2,1024,128]{2,0,1:T(2,128)(2,1)S(1)}, u32[]{:S(2)}, u32[]{:S(2)}) async-start(bf16[2,1024,128]{2,0,1:T(2,128)(2,1)} %copy.128), calls=%async_computation.5 | async-start | bytes 1048576 | tf_op jit(solution)/shard_map/all_to_all | solution.py:162
  294.2 2.0 copy.131
  296.2 20.8 %all-to-all-done.5 = bf16[2,1024,128]{2,0,1:T(2,128)(2,1)S(1)} async-done(((bf16[2,1024,128]{2,0,1:T(2,128)(2,1)}), bf16[2,1024,128]{2,0,1:T(2,128)(2,1)S(1)}, u32[]{:S(2)}, u32[]{:S(2)}) %all-to-all-start.5) | async-done | bytes 524320 | tf_op jit(solution)/shard_map/all_to_all | solution.py:162
  317.0 12.2 %all-to-all-start.6 = ((bf16[2,1024,128]{2,0,1:T(2,128)(2,1)}), bf16[2,1024,128]{2,0,1:T(2,128)(2,1)S(1)}, u32[]{:S(2)}, u32[]{:S(2)}) async-start(bf16[2,1024,128]{2,0,1:T(2,128)(2,1)} %copy.131), calls=%async_computation.6 | async-start | bytes 1048576 | tf_op jit(solution)/shard_map/all_to_all | solution.py:163
  330.3 21.7 %all-to-all-done.6 = bf16[2,1024,128]{2,0,1:T(2,128)(2,1)S(1)} async-done(((bf16[2,1024,128]{2,0,1:T(2,128)(2,1)}), bf16[2,1024,128]{2,0,1:T(2,128)(2,1)S(1)}, u32[]{:S(2)}, u32[]{:S(2)}) %all-to-all-start.6) | async-done | bytes 524320 | tf_op jit(solution)/shard_map/all_to_all | solution.py:163
  352.0 12.2 %all-to-all-start.7 = ((bf16[2,1024,128]{2,0,1:T(2,128)(2,1)}), bf16[2,1024,128]{2,0,1:T(2,128)(2,1)S(1)}, u32[]{:S(2)}, u32[]{:S(2)}) async-start(bf16[2,1024,128]{2,0,1:T(2,128)(2,1)} %copy.134), calls=%async_computation.7 | async-start | bytes 1048576 | tf_op jit(solution)/shard_map/all_to_all | solution.py:164
  365.3 21.7 %all-to-all-done.7 = bf16[2,1024,128]{2,0,1:T(2,128)(2,1)S(1)} async-done(((bf16[2,1024,128]{2,0,1:T(2,128)(2,1)}), bf16[2,1024,128]{2,0,1:T(2,128)(2,1)S(1)}, u32[]{:S(2)}, u32[]{:S(2)}) %all-to-all-start.7) | async-done | bytes 524320 | tf_op jit(solution)/shard_map/all_to_all | solution.py:164
  387.0 12.2 %all-to-all-start.8 = ((bf16[2,1024,128]{2,0,1:T(2,128)(2,1)}), bf16[2,1024,128]{2,0,1:T(2,128)(2,1)S(1)}, u32[]{:S(2)}, u32[]{:S(2)}) async-start(bf16[2,1024,128]{2,0,1:T(2,128)(2,1)} %copy.137), calls=%async_computation.8 | async-start | bytes 1048576 | tf_op jit(solution)/shard_map/all_to_all | solution.py:165
  401.2 64.0 %all-reduce.2 = (f32[2,64]{1,0:T(2,128)S(1)}, f32[2,64]{1,0:T(2,128)S(1)}) all-reduce(f32[2,64]{1,0:T(2,128)S(1)} %reduce_sum.144, f32[2,64]{1,0:T(2,128)S(1)} %reduce_sum.145), channel_id=2, replica_groups=mesh['dp'=32,'seq'=16] {'dp'}, use_global_device_ids=true, to_apply=%region_19.20.clone | all-reduce | flops 256 | bytes 2048
  (258 shorter events, 55.2 us)
Async XLA Ops:
  0.6 19.8 %collective-permute-start.1 = (s32[2,64]{1,0:T(2,128)}, s32[2,64]{1,0:T(2,128)S(1)}, u32[]{:S(2)}, u32[]{:S(2)}) collective-permute-start(s32[2,64]{1,0:T(2,128)} %param.14), channel_id=1, source_target_pairs={{0,256},{16,272},{32,288},{48,304},{64,320},{80,336},{96,352},{112... | collective-permute-start | bytes 1544 | tf_op jit(solution)/shard_map/ppermute | solution.py:17
  6.1 30.7 %collective-permute-start.2 = (bf16[2,64,2048]{2,1,0:T(8,128)(2,1)}, bf16[2,64,2048]{2,1,0:T(8,128)(2,1)S(1)}, u32[]{:S(2)}, u32[]{:S(2)}) collective-permute-start(bf16[2,64,2048]{2,1,0:T(8,128)(2,1)} %param.10), channel_id=1, source_target_pairs={{0,256},{16,272},{32,288},{48,304},{64,320},{80,336},{96,352},{112... | collective-permute-start | bytes 1572872 | tf_op jit(solution)/shard_map/ppermute | solution.py:17
  8.1 28.7 %collective-permute-start.3 = (bf16[2,64,2048]{2,1,0:T(8,128)(2,1)}, bf16[2,64,2048]{2,1,0:T(8,128)(2,1)S(1)}, u32[]{:S(2)}, u32[]{:S(2)}) collective-permute-start(bf16[2,64,2048]{2,1,0:T(8,128)(2,1)} %param.11), channel_id=1, source_target_pairs={{0,256},{16,272},{32,288},{48,304},{64,320},{80,336},{96,352},{112... | collective-permute-start | bytes 1572872 | tf_op jit(solution)/shard_map/ppermute | solution.py:17
  12.9 29.4 %collective-permute-start = (bf16[2,64,2048]{2,1,0:T(8,128)(2,1)}, bf16[2,64,2048]{2,1,0:T(8,128)(2,1)S(1)}, u32[]{:S(2)}, u32[]{:S(2)}) collective-permute-start(bf16[2,64,2048]{2,1,0:T(8,128)(2,1)} %param.12), channel_id=1, source_target_pairs={{0,256},{16,272},{32,288},{48,304},{64,320},{80,336},{96,352},{112... | collective-permute-start | bytes 1572872 | tf_op jit(solution)/shard_map/ppermute | solution.py:17
  14.9 38.8 %collective-permute-start.4 = (bf16[2,64,2048]{2,1,0:T(8,128)(2,1)}, bf16[2,64,2048]{2,1,0:T(8,128)(2,1)}, u32[]{:S(2)}, u32[]{:S(2)}) collective-permute-start(bf16[2,64,2048]{2,1,0:T(8,128)(2,1)} %param.13), channel_id=1, source_target_pairs={{0,256},{16,272},{32,288},{48,304},{64,320},{80,336},{96,352},{112... | collective-permute-start | bytes 1572872 | tf_op jit(solution)/shard_map/ppermute | solution.py:17
  21.9 36.2 %all-to-all-start.1 = ((s32[16,1,128]{2,1,0:T(1,128)}), s32[16,1,128]{2,1,0:T(1,128)S(1)}, u32[]{:S(2)}, u32[]{:S(2)}) async-start(s32[16,1,128]{2,1,0:T(1,128)} %reshape.278), calls=%async_computation.1 | async-start | bytes 16384 | tf_op jit(solution)/shard_map/all_to_all | solution.py:150
  58.1 39.3 %all-to-all-start.4 = ((bf16[16,2,8192]{2,1,0:T(2,128)(2,1)}), bf16[16,2,8192]{2,1,0:T(2,128)(2,1)S(1)}, u32[]{:S(2)}, u32[]{:S(2)}) async-start(bf16[16,2,8192]{2,1,0:T(2,128)(2,1)} %reshape.284), calls=%async_computation.4 | async-start | bytes 1048576 | tf_op jit(solution)/shard_map/all_to_all | solution.py:149
  97.4 35.7 %all-to-all-start.2 = ((bf16[16,2,8192]{2,1,0:T(2,128)(2,1)}), bf16[16,2,8192]{2,1,0:T(2,128)(2,1)S(1)}, u32[]{:S(2)}, u32[]{:S(2)}) async-start(bf16[16,2,8192]{2,1,0:T(2,128)(2,1)} %reshape.280), calls=%async_computation.2 | async-start | bytes 1048576 | tf_op jit(solution)/shard_map/all_to_all | solution.py:146
  110.3 70.1 %copy-start.25 = (f32[2,64]{1,0:T(2,128)S(1)}, f32[2,64]{1,0:T(2,128)}, u32[]{:S(2)}) copy-start(f32[2,64]{1,0:T(2,128)} %param.16) | copy-start | bytes 1540
  133.1 35.0 %all-to-all-start.3 = ((bf16[16,2,8192]{2,1,0:T(2,128)(2,1)}), bf16[16,2,8192]{2,1,0:T(2,128)(2,1)S(1)}, u32[]{:S(2)}, u32[]{:S(2)}) async-start(bf16[16,2,8192]{2,1,0:T(2,128)(2,1)} %reshape.282), calls=%async_computation.3 | async-start | bytes 1048576 | tf_op jit(solution)/shard_map/all_to_all | solution.py:147
  168.1 35.0 %all-to-all-start = ((bf16[16,2,8192]{2,1,0:T(2,128)(2,1)}), bf16[16,2,8192]{2,1,0:T(2,128)(2,1)S(1)}, u32[]{:S(2)}, u32[]{:S(2)}) async-start(bf16[16,2,8192]{2,1,0:T(2,128)(2,1)} %reshape.276), calls=%async_computation | async-start | bytes 1048576 | tf_op jit(solution)/shard_map/all_to_all | solution.py:148
  185.4 20.2 %copy-start.22 = (f32[2,64]{1,0:T(2,128)S(1)}, f32[2,64]{1,0:T(2,128)}, u32[]{:S(2)}) copy-start(f32[2,64]{1,0:T(2,128)} %param.17) | copy-start | bytes 1540
  205.6 12.7 %copy-start.20 = (s32[2,1024]{1,0:T(2,128)}, s32[2,1024]{1,0:T(2,128)S(1)}, u32[]{:S(2)}) copy-start(s32[2,1024]{1,0:T(2,128)S(1)} %get-tuple-element.510) | copy-start | bytes 24580 | tf_op jit(solution)/shard_map/while
  211.8 10.8 %copy-start.4 = (bf16[1,1024,128]{1,2,0:T(8,128)(2,1)}, bf16[1,1024,128]{1,2,0:T(8,128)(2,1)S(1)}, u32[]{:S(2)}) copy-start(bf16[1,1024,128]{1,2,0:T(8,128)(2,1)S(1)} %copy.179) | copy-start | bytes 786436 | tf_op jit(solution)/shard_map/while
  212.7 5.6 %copy-start.8 = (bf16[1024,2,64]{0,2,1:T(8,128)(2,1)}, bf16[1024,2,64]{0,2,1:T(8,128)(2,1)S(1)}, u32[]{:S(2)}) copy-start(bf16[1024,2,64]{0,2,1:T(8,128)(2,1)S(1)} %multiply_convert_fusion.9) | copy-start | bytes 786436 | tf_op jit(solution)/shard_map/while
  218.3 4.3 copy-start.3
  218.3 4.3 copy-start.28
  231.6 2.8 copy-start.5
  231.6 2.8 copy-start.6
  234.4 2.5 copy-start.2
  234.4 2.5 copy-start.27
  237.9 2.3 copy-start.12
  237.9 2.3 copy-start.14
  237.9 2.3 copy-start.26
  238.7 2.2 copy-start.7
  238.7 2.2 copy-start.16
  239.4 3.3 copy-start.21
  242.7 12.7 %copy-start.20 = (s32[2,1024]{1,0:T(2,128)}, s32[2,1024]{1,0:T(2,128)S(1)}, u32[]{:S(2)}) copy-start(s32[2,1024]{1,0:T(2,128)S(1)} %get-tuple-element.510) | copy-start | bytes 24580 | tf_op jit(solution)/shard_map/while
  248.9 10.8 %copy-start.4 = (bf16[1,1024,128]{1,2,0:T(8,128)(2,1)}, bf16[1,1024,128]{1,2,0:T(8,128)(2,1)S(1)}, u32[]{:S(2)}) copy-start(bf16[1,1024,128]{1,2,0:T(8,128)(2,1)S(1)} %copy.179) | copy-start | bytes 786436 | tf_op jit(solution)/shard_map/while
  249.7 5.6 %copy-start.8 = (bf16[1024,2,64]{0,2,1:T(8,128)(2,1)}, bf16[1024,2,64]{0,2,1:T(8,128)(2,1)S(1)}, u32[]{:S(2)}) copy-start(bf16[1024,2,64]{0,2,1:T(8,128)(2,1)S(1)} %multiply_convert_fusion.9) | copy-start | bytes 786436 | tf_op jit(solution)/shard_map/while
  255.3 4.3 copy-start.3
  255.3 4.3 copy-start.28
  268.6 2.8 copy-start.5
  268.6 2.8 copy-start.6
  271.4 2.5 copy-start.2
  271.4 2.5 copy-start.27
  274.9 2.3 copy-start.12
  274.9 2.3 copy-start.14
  274.9 2.3 copy-start.26
  276.5 3.3 copy-start.21
  279.9 49.3 %copy-start.19 = (bf16[2,1024,128]{1,2,0:T(8,128)(2,1)S(1)}, bf16[2,1024,128]{1,2,0:T(8,128)(2,1)}, u32[]{:S(2)}) copy-start(bf16[2,1024,128]{1,2,0:T(8,128)(2,1)} %get-tuple-element.565) | copy-start | bytes 1572868
  279.9 84.3 %copy-start.18 = (bf16[2,1024,128]{1,2,0:T(8,128)(2,1)S(1)}, bf16[2,1024,128]{1,2,0:T(8,128)(2,1)}, u32[]{:S(2)}) copy-start(bf16[2,1024,128]{1,2,0:T(8,128)(2,1)} %get-tuple-element.566) | copy-start | bytes 1572868
  279.9 121.2 %copy-start.32 = (f32[2,2,64]{2,1,0:T(2,128)S(1)}, f32[2,2,64]{2,1,0:T(2,128)}, u32[]{:S(2)}) copy-start(f32[2,2,64]{2,1,0:T(2,128)} %get-tuple-element.568) | copy-start | bytes 3076
  279.9 121.2 %copy-start.35 = (f32[2,2,64]{2,1,0:T(2,128)S(1)}, f32[2,2,64]{2,1,0:T(2,128)}, u32[]{:S(2)}) copy-start(f32[2,2,64]{2,1,0:T(2,128)} %get-tuple-element.567) | copy-start | bytes 3076
  282.0 35.0 %all-to-all-start.5 = ((bf16[2,1024,128]{2,0,1:T(2,128)(2,1)}), bf16[2,1024,128]{2,0,1:T(2,128)(2,1)S(1)}, u32[]{:S(2)}, u32[]{:S(2)}) async-start(bf16[2,1024,128]{2,0,1:T(2,128)(2,1)} %copy.128), calls=%async_computation.5 | async-start | bytes 1048576 | tf_op jit(solution)/shard_map/all_to_all | solution.py:162
  317.0 35.0 %all-to-all-start.6 = ((bf16[2,1024,128]{2,0,1:T(2,128)(2,1)}), bf16[2,1024,128]{2,0,1:T(2,128)(2,1)S(1)}, u32[]{:S(2)}, u32[]{:S(2)}) async-start(bf16[2,1024,128]{2,0,1:T(2,128)(2,1)} %copy.131), calls=%async_computation.6 | async-start | bytes 1048576 | tf_op jit(solution)/shard_map/all_to_all | solution.py:163
  352.0 35.0 %all-to-all-start.7 = ((bf16[2,1024,128]{2,0,1:T(2,128)(2,1)}), bf16[2,1024,128]{2,0,1:T(2,128)(2,1)S(1)}, u32[]{:S(2)}, u32[]{:S(2)}) async-start(bf16[2,1024,128]{2,0,1:T(2,128)(2,1)} %copy.134), calls=%async_computation.7 | async-start | bytes 1048576 | tf_op jit(solution)/shard_map/all_to_all | solution.py:164
  387.0 81.8 %all-to-all-start.8 = ((bf16[2,1024,128]{2,0,1:T(2,128)(2,1)}), bf16[2,1024,128]{2,0,1:T(2,128)(2,1)S(1)}, u32[]{:S(2)}, u32[]{:S(2)}) async-start(bf16[2,1024,128]{2,0,1:T(2,128)(2,1)} %copy.137), calls=%async_computation.8 | async-start | bytes 1048576 | tf_op jit(solution)/shard_map/all_to_all | solution.py:165
  (31 other events, 46.7 us)
where the time goes:
time: 473 us; the launch traced here: 470 us
  waiting for transfers between devices  154 us (33%)
  starting transfers between devices  137 us (29%)
  blocking collectives  64 us (14%)
  local copies, waits for them, and re-layouts  52.7 us (11%)
  matrix products  37.1 us (8%)
  other arithmetic  21 us (4%)
    unnamed x1, blocking collectives  64 us
    all_to_all x1, waiting for transfers between devices, body(): lax.all_to_all(results[1], 'seq', split_axis=1, concat_axis=2, tiled=True)  21.7 us
    all_to_all x1, waiting for transfers between devices, body(): lax.all_to_all(results[2], 'seq', split_axis=1, concat_axis=2, tiled=True)  21.7 us
    all_to_all x1, waiting for transfers between devices, body(): lax.all_to_all(as_sent(results[0]), 'seq', split_axis=1, concat_axis=2, t...  20.8 us
    all_to_all x1, waiting for transfers between devices, body(): lax.all_to_all(key_rows, 'seq', split_axis=2, concat_axis=1, tiled=True)  20.5 us
    all_to_all x1, waiting for transfers between devices, body(): lax.all_to_all(query_rows, 'seq', split_axis=2, concat_axis=1, tiled=True)  20.5 us
    all_to_all x1, waiting for transfers between devices, body(): lax.all_to_all(cotangent, 'seq', split_axis=2, concat_axis=1, tiled=True)  19.8 us
    ppermute x5, starting transfers between devices, from_partner(): return lax.ppermute(value, axis, pairs)  19.1 us
  transfers between devices with their start and end apart: 14, of which 9 were waited for; matrix products, arithmetic and copies ran while one was open for 7% of the time, Pallas kernels for 0%

commit v1 on v0

v1 whole, which is shorter than its diff:
```python
import functools

import jax
import jax.numpy as jnp
from jax import lax
from jax.experimental import pallas as pl
from jax.experimental.pallas import tpu as pltpu
from jax.sharding import PartitionSpec as P

MESH = pl.DeviceIdType.MESH
HEAD_DIM = 64
EPSILON = 1e-06
ROWS = 64
LANES = 128
SCALE = HEAD_DIM ** (-0.5)
MASKED = -1e30
F32 = jnp.float32
BF16 = jnp.bfloat16


def dot(a, b):
    return jnp.dot(a, b, preferred_element_type=F32)


def column(gain):
    row = jnp.concatenate([gain[0:1, :], gain[1:2, :]], axis=1)
    return jnp.transpose(jnp.broadcast_to(row, (LANES, LANES)))[:, 0:1]


def normalize(raw):
    parts = raw.reshape(2, HEAD_DIM, raw.shape[1])
    centred = parts - jnp.mean(parts, axis=1, keepdims=True)
    inv_std = lax.rsqrt(jnp.mean(centred * centred, axis=1, keepdims=True) + EPSILON)
    return (centred * inv_std).reshape(raw.shape), inv_std


def norm_back(grad, unit_rows, inv_std, gain):
    scaled = (grad * gain).reshape(2, HEAD_DIM, grad.shape[1])
    unit = unit_rows.reshape(scaled.shape)
    inner = (
        scaled
        - jnp.mean(scaled, axis=1, keepdims=True)
        - unit * jnp.mean(scaled * unit, axis=1, keepdims=True)
    )
    return (inv_std * inner).reshape(grad.shape)


def fold_lanes(x):
    total = x[:, 0:LANES]
    for start in range(LANES, x.shape[1], LANES):
        total = total + x[:, start : start + LANES]
    return total


def main_kernel(
    nz, ndp, block,
    moved_ref, q_ref, k_ref, v_ref, c_ref, seg_ref, qg_ref, kg_ref,
    ab_ref, gain_ref,
    raw, stage, xrecv, inbuf, outbuf,
    seg_stage, seg_x, seg_all,
    q_unit, k_unit, q_inv, k_inv, q_t, c_t, q_n, c_n, k_n, k_t, v_t, seg_col, seg_row,
    key_acc, value_acc, gain_acc, gain_send, gain_recv,
    load_sem, xs, xr, xsegs, xsegr, zs, zr, segs, segr, outs, outr, gs, gr,
):
    dp, z = lax.axis_index("dp"), lax.axis_index("seq")
    length = nz * ROWS
    lanes = nz * LANES
    partner = lax.rem(dp + ndp // 2, ndp)

    def remote(src, dst, send, recv, device):
        return pltpu.make_async_remote_copy(
            src_ref=src, dst_ref=dst, send_sem=send, recv_sem=recv,
            device_id=device, device_id_type=MESH,
        )

    def arrived(ref, sem):
        pltpu.make_async_copy(ref, ref, sem).wait()

    loads = [
        pltpu.make_async_copy(ref, raw.at[a], load_sem.at[a])
        for a, ref in enumerate((q_ref, k_ref, v_ref, c_ref))
    ]
    for load in loads:
        load.start()

    barrier = pltpu.get_barrier_semaphore()
    for d in range(1, nz):
        pl.semaphore_signal(
            barrier, inc=1, device_id=(dp, lax.rem(z + d, nz)), device_id_type=MESH
        )
    for d in range(1, ndp):
        pl.semaphore_signal(
            barrier, inc=1, device_id=(lax.rem(dp + d, ndp), z), device_id_type=MESH
        )
    pl.semaphore_wait(barrier, nz - 1 + ndp - 1)

    by_distance = sorted(range(1, nz), key=lambda d: (min(d, nz - d), d))

    def send_rows(p, slot):
        for d in by_distance:
            peer = lax.rem(z + d, nz)
            remote(
                stage.at[slot, :, :, pl.ds(pl.multiple_of(peer * LANES, LANES), LANES)],
                inbuf.at[p, :, pl.ds(pl.multiple_of(z * ROWS, ROWS), ROWS), :],
                zs.at[p], zr.at[p], (dp, peer),
            ).start()
        pltpu.make_async_copy(
            stage.at[slot, :, :, pl.ds(pl.multiple_of(z * LANES, LANES), LANES)],
            inbuf.at[p, :, pl.ds(pl.multiple_of(z * ROWS, ROWS), ROWS), :],
            zr.at[p],
        ).start()
        seg_all[p, z] = seg_stage[slot]
        for d in by_distance:
            remote(
                seg_stage.at[slot], seg_all.at[p, z], segs.at[p], segr.at[p],
                (dp, lax.rem(z + d, nz)),
            ).start()

    def send_results(p):
        for d in by_distance:
            peer = lax.rem(z + d, nz)
            remote(
                outbuf.at[p, :, pl.ds(pl.multiple_of(peer * ROWS, ROWS), ROWS), :],
                ab_ref.at[p, :, :, pl.ds(pl.multiple_of(z * LANES, LANES), LANES)],
                outs.at[p], outr.at[p], (dp, peer),
            ).start()
        pltpu.make_async_copy(
            outbuf.at[p, :, pl.ds(pl.multiple_of(z * ROWS, ROWS), ROWS), :],
            ab_ref.at[p, :, :, pl.ds(pl.multiple_of(z * LANES, LANES), LANES)],
            outr.at[p],
        ).start()

    moved = moved_ref[0]
    b_first = moved == 0
    segs_in = seg_ref[...].astype(F32)
    seg0 = jnp.broadcast_to(segs_in[0:1, 0:1], (8, LANES))
    seg1 = jnp.broadcast_to(segs_in[1:2, 0:1], (8, LANES))
    seg_stage[0] = jnp.where(b_first, seg1, seg0)
    seg_stage[1] = jnp.where(b_first, seg0, seg1)
    for a, load in enumerate(loads):
        load.wait()
        stage[1, a] = jnp.where(b_first, raw[a, 0], raw[a, 1])
        stage[0, a] = jnp.where(b_first, raw[a, 1], raw[a, 0])
    send_rows(0, 0)
    trades = []
    for a in range(4):
        trade = remote(stage.at[1, a], xrecv.at[a], xs.at[a], xr.at[a], (partner, z))
        trade.start()
        trades.append(trade)
    seg_trade = remote(seg_stage.at[1], seg_x, xsegs, xsegr, (partner, z))
    seg_trade.start()

    stays = moved == 2
    seg_trade.wait()
    seg_stage[2] = jnp.where(stays, seg_stage[1], seg_x[...])
    for a in range(4):
        trades[a].wait()
        stage[2, a] = jnp.where(stays, stage[1, a], xrecv[a])
    send_rows(1, 2)

    q_gain, k_gain = column(qg_ref[...]), column(kg_ref[...])
    gain_acc[...] = jnp.zeros_like(gain_acc)

    def compute(p):
        top = lax.broadcasted_iota(jnp.int32, (LANES, length), 0) < HEAD_DIM
        left = lax.broadcasted_iota(jnp.int32, (length, LANES), 1) < HEAD_DIM

        def split_down(x):
            return jnp.where(top, x, 0.0).astype(BF16), jnp.where(top, 0.0, x).astype(BF16)

        def split_across(x):
            return jnp.where(left, x, 0.0).astype(BF16), jnp.where(left, 0.0, x).astype(BF16)

        ids = seg_all[p, :, 0:1, :]
        spread = jnp.broadcast_to(ids, (nz, ROWS, LANES)).reshape(length, LANES)
        seg_col[...] = spread
        seg_row[...] = jnp.transpose(spread)[0:8, :]

        unit, inv = normalize(jnp.transpose(inbuf[p, 0].astype(F32)))
        q_unit[...], q_inv[...] = unit, inv
        low = (unit * q_gain).astype(BF16).astype(F32) * SCALE
        q_t[0], q_t[1] = split_down(low)
        q_n[0], q_n[1] = split_across(jnp.transpose(low))

        unit, inv = normalize(jnp.transpose(inbuf[p, 1].astype(F32)))
        k_unit[...], k_inv[...] = unit, inv
        low = (unit * k_gain).astype(BF16).astype(F32)
        k_t[...] = low.astype(BF16)
        k_n[...] = jnp.transpose(low).astype(BF16)

        v_t[...] = jnp.transpose(inbuf[p, 2].astype(F32)).astype(BF16)
        cot = inbuf[p, 3].astype(F32)
        c_n[0], c_n[1] = split_across(cot)
        c_t[0], c_t[1] = split_down(jnp.transpose(cot))
        key_acc[...] = jnp.zeros_like(key_acc)
        value_acc[...] = jnp.zeros_like(value_acc)

        def step(i, carry):
            at = pl.ds(pl.multiple_of(i * block, block), block)
            wide = jnp.concatenate([seg_col[...]] * (block // LANES), axis=1)
            same = wide == seg_row[0:1, at]
            attended, grad = [], []
            for h in range(2):
                head = pl.ds(h * HEAD_DIM, HEAD_DIM)
                scores = jnp.where(same, dot(k_n[...], q_t[h, :, at]), MASKED)
                exponent = jnp.exp(scores - jnp.max(scores, axis=0, keepdims=True))
                weights = exponent * (1.0 / jnp.sum(exponent, axis=0, keepdims=True))
                weights_low = weights.astype(BF16)
                full = dot(v_t[head, :], weights_low)
                delta = jnp.sum(c_t[h, head, at].astype(F32) * full, axis=0, keepdims=True)
                prob_grad = dot(inbuf[p, 2], c_t[h, :, at])
                score_grad = (weights * (prob_grad - delta)).astype(BF16)
                value_acc[...] += dot(weights_low, c_n[h, at, :])
                key_acc[...] += dot(score_grad, q_n[h, at, :])
                attended.append(full)
                grad.append(dot(k_t[head, :], score_grad) * SCALE)
            outbuf[p, 0, at, :] = jnp.transpose(jnp.concatenate(attended, axis=0)).astype(BF16)
            grad = jnp.concatenate(grad, axis=0)
            unit = q_unit[:, at]
            gain_acc[0] += fold_lanes(grad * unit)
            back = norm_back(grad, unit, q_inv[:, :, at], q_gain)
            outbuf[p, 1, at, :] = jnp.transpose(back).astype(BF16)
            return carry

        lax.fori_loop(0, length // block, step, 0)
        outbuf[p, 3] = value_acc[...].astype(BF16)
        grad = jnp.transpose(key_acc[...])
        unit = k_unit[...]
        gain_acc[1] += fold_lanes(grad * unit)
        back = norm_back(grad, unit, k_inv[...], k_gain)
        outbuf[p, 2] = jnp.transpose(back).astype(BF16)

    for p in range(2):
        arrived(inbuf.at[p], zr.at[p])
        arrived(seg_all.at[p, pl.ds(0, nz - 1)], segr.at[p])
        compute(p)
        send_results(p)

    rows = [jnp.sum(jnp.transpose(gain_acc[i]), axis=0, keepdims=True) for i in range(2)]
    pick = lax.broadcasted_iota(jnp.int32, (8, LANES), 0)
    gain_send[...] = jnp.where(pick == 0, rows[0], jnp.where(pick == 1, rows[1], 0.0))
    gain_recv[dp] = gain_send[...]
    for d in range(1, ndp):
        remote(gain_send, gain_recv.at[dp], gs, gr, (lax.rem(dp + d, ndp), z)).start()
    arrived(gain_recv.at[pl.ds(0, ndp - 1)], gr)
    gain_ref[...] = jnp.sum(gain_recv[...], axis=0)

    for p in range(2):
        arrived(ab_ref.at[p], outr.at[p])
        arrived(stage.at[2 * p, :, :, pl.ds(0, lanes - LANES)], zs.at[p])
        arrived(seg_all.at[p, pl.ds(0, nz - 1)], segs.at[p])
        arrived(outbuf.at[p, :, pl.ds(0, length - ROWS), :], outs.at[p])
    arrived(gain_recv.at[pl.ds(0, ndp - 1)], gs)


def place_kernel(moved_ref, ab_ref, gain_ref, out0, out1, out2, out3, gq_ref, gk_ref, sem):
    dp = lax.axis_index("dp")
    b_slot = jnp.where(moved_ref[0] == 0, 0, 1)
    copies = []
    for a, out in enumerate((out0, out1, out2, out3)):
        for p in range(2):
            slot = 1 - b_slot if p == 0 else b_slot
            copies.append(pltpu.make_async_copy(ab_ref.at[p, a], out.at[slot], sem.at[a, p]))
            copies[-1].start()
    lane = lax.broadcasted_iota(jnp.int32, (1, LANES), 1)
    down = lax.broadcasted_iota(jnp.int32, (2, 2), 0)
    across = lax.broadcasted_iota(jnp.int32, (2, 2), 1)
    for i, ref in enumerate((gq_ref, gk_ref)):
        row = gain_ref[i : i + 1, :]
        total = jnp.zeros((2, 2), F32)
        for h in range(2):
            for j in range(2):
                chosen = lane == h * HEAD_DIM + 2 * dp + j
                value = jnp.sum(jnp.where(chosen, row, 0.0), axis=1, keepdims=True)
                total = jnp.where((down == h) & (across == j), value, total)
        ref[...] = total
    for copy in copies:
        copy.wait()


def body(nz, ndp, q, k, v, c, seg, moved, q_gain, k_gain):
    length, lanes = nz * ROWS, nz * LANES
    block = min(256, length)
    anywhere = pl.BlockSpec(memory_space=pl.ANY)
    vmem = pl.BlockSpec(memory_space=pltpu.VMEM)
    smem = pl.BlockSpec(memory_space=pltpu.SMEM)
    dma = pltpu.SemaphoreType.DMA
    ab, gains = pl.pallas_call(
        functools.partial(main_kernel, nz, ndp, block),
        out_shape=(
            jax.ShapeDtypeStruct((2, 4, ROWS, lanes), BF16),
            jax.ShapeDtypeStruct((8, LANES), F32),
        ),
        in_specs=[smem] + [anywhere] * 4 + [vmem] * 3,
        out_specs=(anywhere, vmem),
        scratch_shapes=[
            pltpu.VMEM((4, 2, ROWS, lanes), BF16),
            pltpu.VMEM((3, 4, ROWS, lanes), BF16),
            pltpu.VMEM((4, ROWS, lanes), BF16),
            pltpu.VMEM((2, 4, length, LANES), BF16),
            pltpu.VMEM((2, 4, length, LANES), BF16),
            pltpu.VMEM((3, 8, LANES), F32),
            pltpu.VMEM((8, LANES), F32),
            pltpu.VMEM((2, nz, 8, LANES), F32),
            pltpu.VMEM((LANES, length), F32),
            pltpu.VMEM((LANES, length), F32),
            pltpu.VMEM((2, 1, length), F32),
            pltpu.VMEM((2, 1, length), F32),
            pltpu.VMEM((2, LANES, length), BF16),
            pltpu.VMEM((2, LANES, length), BF16),
            pltpu.VMEM((2, length, LANES), BF16),
            pltpu.VMEM((2, length, LANES), BF16),
            pltpu.VMEM((length, LANES), BF16),
            pltpu.VMEM((LANES, length), BF16),
            pltpu.VMEM((LANES, length), BF16),
            pltpu.VMEM((length, LANES), F32),
            pltpu.VMEM((8, length), F32),
            pltpu.VMEM((length, LANES), F32),
            pltpu.VMEM((length, LANES), F32),
            pltpu.VMEM((2, LANES, LANES), F32),
            pltpu.VMEM((8, LANES), F32),
            pltpu.VMEM((ndp, 8, LANES), F32),
            dma((4,)),
            dma((4,)), dma((4,)), dma(()), dma(()),
            dma((2,)), dma((2,)), dma((2,)), dma((2,)),
            dma((2,)), dma((2,)), dma(()), dma(()),
        ],
        compiler_params=pltpu.CompilerParams(
            collective_id=0, has_side_effects=True, vmem_limit_bytes=48 << 20
        ),
        name="attend",
    )(moved, q, k, v, c, seg, q_gain, k_gain)
    rows = jax.ShapeDtypeStruct((2, ROWS, lanes), BF16)
    small = jax.ShapeDtypeStruct((2, 2), F32)
    return pl.pallas_call(
        place_kernel,
        out_shape=(rows, rows, rows, rows, small, small),
        in_specs=[smem, anywhere, vmem],
        out_specs=(anywhere,) * 4 + (vmem, vmem),
        scratch_shapes=[dma((4, 2))],
        name="place",
    )(moved, ab, gains)


def solution(mesh):
    return jax.shard_map(
        functools.partial(body, mesh.shape["seq"], mesh.shape["dp"]),
        mesh=mesh,
        in_specs=(
            P("dp", "seq", None),
            P("dp", "seq", None),
            P("dp", "seq", None),
            P("dp", "seq", None),
            P("dp", "seq"),
            P("dp"),
            P("seq", None),
            P("seq", None),
        ),
        out_specs=(
            P("dp", "seq", None),
            P("dp", "seq", None),
            P("dp", "seq", None),
            P("dp", "seq", None),
            P("seq", "dp"),
            P("seq", "dp"),
        ),
        check_vma=False,
    )
```

time: 473 us -> 282 us (0.60)
  Pallas kernels: 0 us -> 272 us
  waiting for transfers between devices: 154 us -> 0 us
  starting transfers between devices: 137 us -> 0 us
  blocking collectives: 64 us -> 0 us
  local copies, waits for them, and re-layouts: 52.7 us -> 8.12 us
  matrix products: 37.1 us -> 0 us
  other arithmetic: 21 us -> 0 us
    pallas_call x0 -> x2, Pallas kernels: none -> 272 us  [the longest x1 206 us: body(): pl.pallas_call(functools.partial(main_kernel, nz, ndp, block), out_shape=...]
    all_to_all x9 -> x0, waiting for transfers between devices: 138 us -> none  [the longest x1 21.7 us: body(): lax.all_to_all(results[1], 'seq', split_axis=1, concat_axis=2, tiled=True)]
    all_to_all x9 -> x0, starting transfers between devices: 118 us -> none  [the longest x1 17.3 us: body(): lax.all_to_all(cotangent, 'seq', split_axis=2, concat_axis=1, tiled=True)]
    unnamed x1 -> x0, blocking collectives: 64 us -> none
    ppermute x5 -> x0, starting transfers between devices: 19.1 us -> none  [from_partner(): return lax.ppermute(value, axis, pairs)]
    sub x4 -> x0, matrix products: 19 us -> none  [pack_work(): exponent = jnp.exp(scores - row_max)]
    dot_general x20 -> x0, matrix products: 18.1 us -> none  [the longest x4 4.43 us: pack_work(): jnp.einsum('hqk,khd->qhd', score_grad, key_norm, preferred_element_type=j...]
    ppermute x5 -> x0, waiting for transfers between devices: 16.1 us -> none  [from_partner(): return lax.ppermute(value, axis, pairs)]
  transfers between devices with their start and end apart: 14 -> 0, of which waited for: 9 -> 0; matrix products, arithmetic and copies ran while one was open for 7% -> 0% of each run, Pallas kernels for 0% -> 0%
where the time goes in v1:
time: 282 us
  Pallas kernels  272 us (96%)
  local copies, waits for them, and re-layouts  8.12 us (3%)
    pallas_call x1, Pallas kernels, body(): pl.pallas_call(functools.partial(main_kernel, nz, ndp, block), out_shape=...  206 us
    pallas_call x1, Pallas kernels, body(): pl.pallas_call(place_kernel, out_shape=(rows, rows, rows, rows, small, sm...  65.9 us
    unnamed x18, local copies, waits for them, and re-layouts  8.12 us

profile of v1, /device:TPU:1, one launch (start us, length us, event | category | flops | bytes accessed | tf_op | source)
XLA Modules:
  0.0 281.9 jit_solution(16135209932935083338)
XLA Ops:
  1.3 0.0 copy-start.1
  1.3 1.0 copy-done.1
  2.3 0.0 copy-start.2
  2.3 1.0 copy-done.2
  3.4 0.0 copy-start.3
  3.4 1.0 copy-done.3
  4.4 0.0 copy-start.4
  4.4 1.0 copy-done.4
  5.4 0.0 copy-start.6
  5.5 0.7 copy-done.6
  6.1 0.0 copy-start.7
  6.1 0.7 copy-done.7
  6.8 0.0 copy-start.8
  6.8 0.7 copy-done.8
  7.5 206.5 %attend.1 = (bf16[2,4,64,2048]{3,2,1,0:T(8,128)(2,1)S(1)}, f32[8,128]{1,0:T(8,128)S(1)}) custom-call(s32[1]{0:T(128)S(6)} %copy.14.moved_ref, bf16[2,64,2048]{2,1,0:T(8,128)(2,1)S(1)} %copy-done.1, bf16[2,64,2048]{2,1,0:T(8,128)(2,1)S(1)} %copy-done.2, bf16[2,64,2048]{2,1,0:T(8,128)(2,1)S(1)} %copy-done.3, bf16[2,64,2048]{2,1,0:T(8,128)(2,1)S(1)} %copy-done.4, ...), custom_call_target="tpu_custom_call" | custom-call | tf_op jit(solution)/shard_map/attend/pallas_call | solution.py:288
  214.0 0.0 copy-start
  214.0 1.3 copy-done
  215.3 0.0 copy-start.5
  215.3 0.6 copy-done.5
  215.9 65.9 %place.1 = (bf16[2,64,2048]{2,1,0:T(8,128)(2,1)}, bf16[2,64,2048]{2,1,0:T(8,128)(2,1)}, bf16[2,64,2048]{2,1,0:T(8,128)(2,1)}, bf16[2,64,2048]{2,1,0:T(8,128)(2,1)}, f32[2,2]{1,0:T(2,128)}, /*index=5*/f32[2,2]{1,0:T(2,128)}) custom-call(s32[1]{0:T(128)S(6)} %copy.14.moved_ref, bf16[2,4,64,2048]{3,2,1,0:T(8,128)(2,1)} %copy-done, f32[8,128]{1,0:T(8,128)} %copy-done.5), custom_call_target="tpu_custom_call" | custom-call | tf_op jit(solution)/shard_map/place/pallas_call | solution.py:335
Async XLA Ops:
  1.3 1.0 copy-start.1
  2.3 1.0 copy-start.2
  3.4 1.0 copy-start.3
  4.4 1.0 copy-start.4
  5.4 0.7 copy-start.6
  6.1 0.7 copy-start.7
  6.8 0.7 copy-start.8
  214.0 1.3 copy-start
  215.3 0.6 copy-start.5

commit v2 on v1

--- a/solution.py
+++ b/solution.py
@@ -54,9 +54,9 @@
 
 def main_kernel(
     nz, ndp, block,
-    moved_ref, q_ref, k_ref, v_ref, c_ref, seg_ref, qg_ref, kg_ref,
+    moved_ref, q_ref, k_ref, v_ref, c_ref, seg_hbm, qg_hbm, kg_hbm,
     ab_ref, gain_ref,
-    raw, stage, xrecv, inbuf, outbuf,
+    raw, seg_ref, qg_ref, kg_ref, stage, xrecv, inbuf, outbuf,
     seg_stage, seg_x, seg_all,
     q_unit, k_unit, q_inv, k_inv, q_t, c_t, q_n, c_n, k_n, k_t, v_t, seg_col, seg_row,
     key_acc, value_acc, gain_acc, gain_send, gain_recv,
@@ -76,39 +76,37 @@
     def arrived(ref, sem):
         pltpu.make_async_copy(ref, ref, sem).wait()
 
+    pairs = [(ref, raw.at[a]) for a, ref in enumerate((q_ref, k_ref, v_ref, c_ref))]
+    pairs += [(seg_hbm, seg_ref), (qg_hbm, qg_ref), (kg_hbm, kg_ref)]
     loads = [
-        pltpu.make_async_copy(ref, raw.at[a], load_sem.at[a])
-        for a, ref in enumerate((q_ref, k_ref, v_ref, c_ref))
+        pltpu.make_async_copy(src, dst, load_sem.at[i]) for i, (src, dst) in enumerate(pairs)
     ]
     for load in loads:
         load.start()
 
+    by_distance = sorted(range(1, nz), key=lambda d: (-min(d, nz - d), d))
+
+    bits = [1 << i for i in range(ndp.bit_length() - 1)]
+    across = [dp + bit * (1 - 2 * lax.rem(dp // bit, 2)) for bit in bits]
     barrier = pltpu.get_barrier_semaphore()
-    for d in range(1, nz):
-        pl.semaphore_signal(
-            barrier, inc=1, device_id=(dp, lax.rem(z + d, nz)), device_id_type=MESH
-        )
-    for d in range(1, ndp):
-        pl.semaphore_signal(
-            barrier, inc=1, device_id=(lax.rem(dp + d, ndp), z), device_id_type=MESH
-        )
-    pl.semaphore_wait(barrier, nz - 1 + ndp - 1)
-
-    by_distance = sorted(range(1, nz), key=lambda d: (min(d, nz - d), d))
-
-    def send_rows(p, slot):
+    for peer in [(dp, lax.rem(z + d, nz)) for d in by_distance] + [(g, z) for g in across]:
+        pl.semaphore_signal(barrier, inc=1, device_id=peer, device_id_type=MESH)
+
+    def send_rows(p, slot, arrays):
         for d in by_distance:
             peer = lax.rem(z + d, nz)
             remote(
-                stage.at[slot, :, :, pl.ds(pl.multiple_of(peer * LANES, LANES), LANES)],
-                inbuf.at[p, :, pl.ds(pl.multiple_of(z * ROWS, ROWS), ROWS), :],
+                stage.at[slot, arrays, :, pl.ds(pl.multiple_of(peer * LANES, LANES), LANES)],
+                inbuf.at[p, arrays, pl.ds(pl.multiple_of(z * ROWS, ROWS), ROWS), :],
                 zs.at[p], zr.at[p], (dp, peer),
             ).start()
         pltpu.make_async_copy(
-            stage.at[slot, :, :, pl.ds(pl.multiple_of(z * LANES, LANES), LANES)],
-            inbuf.at[p, :, pl.ds(pl.multiple_of(z * ROWS, ROWS), ROWS), :],
+            stage.at[slot, arrays, :, pl.ds(pl.multiple_of(z * LANES, LANES), LANES)],
+            inbuf.at[p, arrays, pl.ds(pl.multiple_of(z * ROWS, ROWS), ROWS), :],
             zr.at[p],
         ).start()
+
+    def send_ids(p, slot):
         seg_all[p, z] = seg_stage[slot]
         for d in by_distance:
             remote(
@@ -117,13 +115,17 @@
             ).start()
 
     def send_results(p):
-        for d in by_distance:
-            peer = lax.rem(z + d, nz)
+        def put(peer, arrays):
             remote(
-                outbuf.at[p, :, pl.ds(pl.multiple_of(peer * ROWS, ROWS), ROWS), :],
-                ab_ref.at[p, :, :, pl.ds(pl.multiple_of(z * LANES, LANES), LANES)],
+                outbuf.at[p, arrays, pl.ds(pl.multiple_of(peer * ROWS, ROWS), ROWS), :],
+                ab_ref.at[p, arrays, :, pl.ds(pl.multiple_of(z * LANES, LANES), LANES)],
                 outs.at[p], outr.at[p], (dp, peer),
             ).start()
+
+        for d in by_distance:
+            put(lax.rem(z + d, nz), pl.ds(0, 3))
+        for j in range(nz - 1):
+            put(j + jnp.where(j >= z, 1, 0), pl.ds(3, 1))
         pltpu.make_async_copy(
             outbuf.at[p, :, pl.ds(pl.multiple_of(z * ROWS, ROWS), ROWS), :],
             ab_ref.at[p, :, :, pl.ds(pl.multiple_of(z * LANES, LANES), LANES)],
@@ -132,23 +134,27 @@
 
     moved = moved_ref[0]
     b_first = moved == 0
+    pl.semaphore_wait(barrier, nz - 1 + len(bits))
+    for a in range(4):
+        loads[a].wait()
+        stage[0, a] = jnp.where(b_first, raw[a, 1], raw[a, 0])
+        send_rows(0, 0, pl.ds(a, 1))
+    trades = []
+    for a in range(4):
+        stage[1, a] = jnp.where(b_first, raw[a, 0], raw[a, 1])
+        trade = remote(stage.at[1, a], xrecv.at[a], xs.at[a], xr.at[a], (partner, z))
+        trade.start()
+        trades.append(trade)
+    for load in loads[4:]:
+        load.wait()
     segs_in = seg_ref[...].astype(F32)
     seg0 = jnp.broadcast_to(segs_in[0:1, 0:1], (8, LANES))
     seg1 = jnp.broadcast_to(segs_in[1:2, 0:1], (8, LANES))
     seg_stage[0] = jnp.where(b_first, seg1, seg0)
     seg_stage[1] = jnp.where(b_first, seg0, seg1)
-    for a, load in enumerate(loads):
-        load.wait()
-        stage[1, a] = jnp.where(b_first, raw[a, 0], raw[a, 1])
-        stage[0, a] = jnp.where(b_first, raw[a, 1], raw[a, 0])
-    send_rows(0, 0)
-    trades = []
-    for a in range(4):
-        trade = remote(stage.at[1, a], xrecv.at[a], xs.at[a], xr.at[a], (partner, z))
-        trade.start()
-        trades.append(trade)
     seg_trade = remote(seg_stage.at[1], seg_x, xsegs, xsegr, (partner, z))
     seg_trade.start()
+    send_ids(0, 0)
 
     stays = moved == 2
     seg_trade.wait()
@@ -156,7 +162,8 @@
     for a in range(4):
         trades[a].wait()
         stage[2, a] = jnp.where(stays, stage[1, a], xrecv[a])
-    send_rows(1, 2)
+    send_rows(1, 2, pl.ds(0, 4))
+    send_ids(1, 2)
 
     q_gain, k_gain = column(qg_ref[...]), column(kg_ref[...])
     gain_acc[...] = jnp.zeros_like(gain_acc)
@@ -238,30 +245,43 @@
 
     rows = [jnp.sum(jnp.transpose(gain_acc[i]), axis=0, keepdims=True) for i in range(2)]
     pick = lax.broadcasted_iota(jnp.int32, (8, LANES), 0)
-    gain_send[...] = jnp.where(pick == 0, rows[0], jnp.where(pick == 1, rows[1], 0.0))
-    gain_recv[dp] = gain_send[...]
-    for d in range(1, ndp):
-        remote(gain_send, gain_recv.at[dp], gs, gr, (lax.rem(dp + d, ndp), z)).start()
-    arrived(gain_recv.at[pl.ds(0, ndp - 1)], gr)
-    gain_ref[...] = jnp.sum(gain_recv[...], axis=0)
+    total = jnp.where(pick == 0, rows[0], jnp.where(pick == 1, rows[1], 0.0))
+    for i, group in enumerate(across):
+        gain_send[i] = total
+        swap = remote(gain_send.at[i], gain_recv.at[i], gs.at[i], gr.at[i], (group, z))
+        swap.start()
+        swap.wait()
+        total = total + gain_recv[i]
+    gain_ref[...] = total
 
     for p in range(2):
         arrived(ab_ref.at[p], outr.at[p])
         arrived(stage.at[2 * p, :, :, pl.ds(0, lanes - LANES)], zs.at[p])
         arrived(seg_all.at[p, pl.ds(0, nz - 1)], segs.at[p])
         arrived(outbuf.at[p, :, pl.ds(0, length - ROWS), :], outs.at[p])
-    arrived(gain_recv.at[pl.ds(0, ndp - 1)], gs)
-
-
-def place_kernel(moved_ref, ab_ref, gain_ref, out0, out1, out2, out3, gq_ref, gk_ref, sem):
+
+
+def place_kernel(
+    moved_ref, ab_ref, gain_ref, out0, out1, out2, out3, gq_ref, gk_ref, held, in_sem, out_sem
+):
     dp = lax.axis_index("dp")
     b_slot = jnp.where(moved_ref[0] == 0, 0, 1)
-    copies = []
-    for a, out in enumerate((out0, out1, out2, out3)):
-        for p in range(2):
-            slot = 1 - b_slot if p == 0 else b_slot
-            copies.append(pltpu.make_async_copy(ab_ref.at[p, a], out.at[slot], sem.at[a, p]))
-            copies[-1].start()
+    pairs = [(a, p) for p in range(2) for a in range(4)]
+    outs = (out0, out1, out2, out3)
+    loads = [
+        pltpu.make_async_copy(ab_ref.at[p, a], held.at[p, a], in_sem.at[p, a]) for a, p in pairs
+    ]
+    stores = [
+        pltpu.make_async_copy(
+            held.at[p, a], outs[a].at[1 - b_slot if p == 0 else b_slot], out_sem.at[p, a]
+        )
+        for a, p in pairs
+    ]
+    for load in loads:
+        load.start()
+    for load, store in zip(loads, stores):
+        load.wait()
+        store.start()
     lane = lax.broadcasted_iota(jnp.int32, (1, LANES), 1)
     down = lax.broadcasted_iota(jnp.int32, (2, 2), 0)
     across = lax.broadcasted_iota(jnp.int32, (2, 2), 1)
@@ -274,13 +294,14 @@
                 value = jnp.sum(jnp.where(chosen, row, 0.0), axis=1, keepdims=True)
                 total = jnp.where((down == h) & (across == j), value, total)
         ref[...] = total
-    for copy in copies:
-        copy.wait()
+    for store in stores:
+        store.wait()
 
 
 def body(nz, ndp, q, k, v, c, seg, moved, q_gain, k_gain):
     length, lanes = nz * ROWS, nz * LANES
     block = min(256, length)
+    hops = ndp.bit_length() - 1
     anywhere = pl.BlockSpec(memory_space=pl.ANY)
     vmem = pl.BlockSpec(memory_space=pltpu.VMEM)
     smem = pl.BlockSpec(memory_space=pltpu.SMEM)
@@ -291,10 +312,13 @@
             jax.ShapeDtypeStruct((2, 4, ROWS, lanes), BF16),
             jax.ShapeDtypeStruct((8, LANES), F32),
         ),
-        in_specs=[smem] + [anywhere] * 4 + [vmem] * 3,
+        in_specs=[smem] + [pl.BlockSpec(memory_space=pltpu.HBM)] * 7,
         out_specs=(anywhere, vmem),
         scratch_shapes=[
             pltpu.VMEM((4, 2, ROWS, lanes), BF16),
+            pltpu.VMEM((2, ROWS), jnp.int32),
+            pltpu.VMEM((2, HEAD_DIM), F32),
+            pltpu.VMEM((2, HEAD_DIM), F32),
             pltpu.VMEM((3, 4, ROWS, lanes), BF16),
             pltpu.VMEM((4, ROWS, lanes), BF16),
             pltpu.VMEM((2, 4, length, LANES), BF16),
@@ -318,15 +342,15 @@
             pltpu.VMEM((length, LANES), F32),
             pltpu.VMEM((length, LANES), F32),
             pltpu.VMEM((2, LANES, LANES), F32),
-            pltpu.VMEM((8, LANES), F32),
-            pltpu.VMEM((ndp, 8, LANES), F32),
-            dma((4,)),
+            pltpu.VMEM((hops, 8, LANES), F32),
+            pltpu.VMEM((hops, 8, LANES), F32),
+            dma((7,)),
             dma((4,)), dma((4,)), dma(()), dma(()),
             dma((2,)), dma((2,)), dma((2,)), dma((2,)),
-            dma((2,)), dma((2,)), dma(()), dma(()),
+            dma((2,)), dma((2,)), dma((hops,)), dma((hops,)),
         ],
         compiler_params=pltpu.CompilerParams(
-            collective_id=0, has_side_effects=True, vmem_limit_bytes=48 << 20
+            collective_id=0, has_side_effects=True, vmem_limit_bytes=60 << 20
         ),
         name="attend",
     )(moved, q, k, v, c, seg, q_gain, k_gain)
@@ -337,7 +361,8 @@
         out_shape=(rows, rows, rows, rows, small, small),
         in_specs=[smem, anywhere, vmem],
         out_specs=(anywhere,) * 4 + (vmem, vmem),
-        scratch_shapes=[dma((4, 2))],
+        scratch_shapes=[pltpu.VMEM((2, 4, ROWS, lanes), BF16), dma((2, 4)), dma((2, 4))],
+        compiler_params=pltpu.CompilerParams(vmem_limit_bytes=60 << 20),
         name="place",
     )(moved, ab, gains)
 

time: 282 us -> 205 us (0.73)
  Pallas kernels: 272 us -> 201 us
  local copies, waits for them, and re-layouts: 8.12 us -> 0 us
    pallas_call x1, Pallas kernels: 65.9 us -> 3.64 us  [body(): pl.pallas_call(place_kernel, out_shape=(rows, rows, rows, rows, small, sm...]
    pallas_call x1, Pallas kernels: 206 us -> 197 us  [body(): pl.pallas_call(functools.partial(main_kernel, nz, ndp, block), out_shape=...]
    unnamed x18 -> x0, local copies, waits for them, and re-layouts: 8.12 us -> none
where the time goes in v2:
time: 205 us; the launch traced here: 202 us
  Pallas kernels  201 us (98%)
    pallas_call x1, Pallas kernels, body(): pl.pallas_call(functools.partial(main_kernel, nz, ndp, block), out_shape=...  197 us

profile of v2, /device:TPU:1, one launch (start us, length us, event | category | flops | bytes accessed | tf_op | source)
XLA Modules:
  0.0 202.2 jit_solution(2721060318602818247)
XLA Ops:
  1.3 197.2 %attend.1 = (bf16[2,4,64,2048]{3,2,1,0:T(8,128)(2,1)}, f32[8,128]{1,0:T(8,128)}) custom-call(s32[1]{0:T(128)S(6)} %copy.14.moved_ref, bf16[2,64,2048]{2,1,0:T(8,128)(2,1)} %q_ref.1, bf16[2,64,2048]{2,1,0:T(8,128)(2,1)} %k_ref.1, bf16[2,64,2048]{2,1,0:T(8,128)(2,1)} %v_ref.1, bf16[2,64,2048]{2,1,0:T(8,128)(2,1)} %c_ref.1, s32[2,64]{1,0:T(2,128)} %seg_hbm.1, ...), custom_call_target="tpu_custom_call" | custom-call | tf_op jit(solution)/shard_map/attend/pallas_call | solution.py:309
  198.5 3.6 %place.1 = (bf16[2,64,2048]{2,1,0:T(8,128)(2,1)}, bf16[2,64,2048]{2,1,0:T(8,128)(2,1)}, bf16[2,64,2048]{2,1,0:T(8,128)(2,1)}, bf16[2,64,2048]{2,1,0:T(8,128)(2,1)}, f32[2,2]{1,0:T(2,128)}, /*index=5*/f32[2,2]{1,0:T(2,128)}) custom-call(s32[1]{0:T(128)S(6)} %copy.14.moved_ref, bf16[2,4,64,2048]{3,2,1,0:T(8,128)(2,1)} %get-tuple-element.8.ab_ref, ...), custom_call_target="tpu_custom_call" | custom-call | tf_op jit(solution)/shard_map/place/pallas_call | solution.py:359

commit v3 on v2

--- a/solution.py
+++ b/solution.py
@@ -54,13 +54,13 @@
 
 def main_kernel(
     nz, ndp, block,
-    moved_ref, q_ref, k_ref, v_ref, c_ref, seg_hbm, qg_hbm, kg_hbm,
+    moved_hbm, q_ref, k_ref, v_ref, c_ref, seg_hbm, qg_hbm, kg_hbm,
     ab_ref, gain_ref,
-    raw, seg_ref, qg_ref, kg_ref, stage, xrecv, inbuf, outbuf,
+    raw, moved_ref, seg_ref, qg_ref, kg_ref, stage, xrecv, inbuf, outbuf,
     seg_stage, seg_x, seg_all,
     q_unit, k_unit, q_inv, k_inv, q_t, c_t, q_n, c_n, k_n, k_t, v_t, seg_col, seg_row,
-    key_acc, value_acc, gain_acc, gain_send, gain_recv,
-    load_sem, xs, xr, xsegs, xsegr, zs, zr, segs, segr, outs, outr, gs, gr,
+    key_acc, value_acc, gain_acc, gain_send, gain_recv, gain_sum,
+    known, load_sem, xs, xr, xsegs, xsegr, zs, zr, segs, segr, outs, outr, gs, gr,
 ):
     dp, z = lax.axis_index("dp"), lax.axis_index("seq")
     length = nz * ROWS
@@ -77,32 +77,42 @@
         pltpu.make_async_copy(ref, ref, sem).wait()
 
     pairs = [(ref, raw.at[a]) for a, ref in enumerate((q_ref, k_ref, v_ref, c_ref))]
-    pairs += [(seg_hbm, seg_ref), (qg_hbm, qg_ref), (kg_hbm, kg_ref)]
+    pairs += [(seg_hbm, seg_ref), (qg_hbm, qg_ref), (kg_hbm, kg_ref), (moved_hbm, moved_ref)]
     loads = [
         pltpu.make_async_copy(src, dst, load_sem.at[i]) for i, (src, dst) in enumerate(pairs)
     ]
-    for load in loads:
+    for load in [loads[-1]] + loads[:-1]:
         load.start()
 
     by_distance = sorted(range(1, nz), key=lambda d: (-min(d, nz - d), d))
 
     bits = [1 << i for i in range(ndp.bit_length() - 1)]
     across = [dp + bit * (1 - 2 * lax.rem(dp // bit, 2)) for bit in bits]
+    beside = [(dp, lax.rem(z + 1, nz)), (dp, lax.rem(z + nz - 1, nz))]
     barrier = pltpu.get_barrier_semaphore()
-    for peer in [(dp, lax.rem(z + d, nz)) for d in by_distance] + [(g, z) for g in across]:
+    for peer in beside + [(g, z) for g in across]:
         pl.semaphore_signal(barrier, inc=1, device_id=peer, device_id_type=MESH)
 
-    def send_rows(p, slot, arrays):
-        for d in by_distance:
+    def tell(k):
+        for peer in beside:
+            pl.semaphore_signal(known.at[k - 1], inc=1, device_id=peer, device_id_type=MESH)
+
+    def pair(k):
+        return [k, nz - k] if k < nz - k else [k]
+
+    def send_rows(p, slot, arrays, distances):
+        for d in distances:
             peer = lax.rem(z + d, nz)
             remote(
                 stage.at[slot, arrays, :, pl.ds(pl.multiple_of(peer * LANES, LANES), LANES)],
                 inbuf.at[p, arrays, pl.ds(pl.multiple_of(z * ROWS, ROWS), ROWS), :],
                 zs.at[p], zr.at[p], (dp, peer),
             ).start()
+
+    def keep_rows(p, slot):
         pltpu.make_async_copy(
-            stage.at[slot, arrays, :, pl.ds(pl.multiple_of(z * LANES, LANES), LANES)],
-            inbuf.at[p, arrays, pl.ds(pl.multiple_of(z * ROWS, ROWS), ROWS), :],
+            stage.at[slot, :, :, pl.ds(pl.multiple_of(z * LANES, LANES), LANES)],
+            inbuf.at[p, :, pl.ds(pl.multiple_of(z * ROWS, ROWS), ROWS), :],
             zr.at[p],
         ).start()
 
@@ -115,37 +125,57 @@
             ).start()
 
     def send_results(p):
-        def put(peer, arrays):
+        def put(peer):
             remote(
-                outbuf.at[p, arrays, pl.ds(pl.multiple_of(peer * ROWS, ROWS), ROWS), :],
-                ab_ref.at[p, arrays, :, pl.ds(pl.multiple_of(z * LANES, LANES), LANES)],
+                outbuf.at[p, :, pl.ds(pl.multiple_of(peer * ROWS, ROWS), ROWS), :],
+                ab_ref.at[p, :, :, pl.ds(pl.multiple_of(z * LANES, LANES), LANES)],
                 outs.at[p], outr.at[p], (dp, peer),
             ).start()
 
+        first = nz * 7 // 16
+        for peer in range(first):
+
+            @pl.when(z != peer)
+            def _():
+                put(peer)
+
         for d in by_distance:
-            put(lax.rem(z + d, nz), pl.ds(0, 3))
-        for j in range(nz - 1):
-            put(j + jnp.where(j >= z, 1, 0), pl.ds(3, 1))
+            peer = lax.rem(z + d, nz)
+
+            @pl.when(peer >= first)
+            def _():
+                put(peer)
+
         pltpu.make_async_copy(
             outbuf.at[p, :, pl.ds(pl.multiple_of(z * ROWS, ROWS), ROWS), :],
             ab_ref.at[p, :, :, pl.ds(pl.multiple_of(z * LANES, LANES), LANES)],
             outr.at[p],
         ).start()
 
+    loads[-1].wait()
     moved = moved_ref[0]
     b_first = moved == 0
-    pl.semaphore_wait(barrier, nz - 1 + len(bits))
+    pl.semaphore_wait(barrier, 2 + len(bits))
+    far = nz // 2
+    if far > 1:
+        tell(1)
     for a in range(4):
         loads[a].wait()
         stage[0, a] = jnp.where(b_first, raw[a, 1], raw[a, 0])
-        send_rows(0, 0, pl.ds(a, 1))
+        send_rows(0, 0, pl.ds(a, 1), pair(1))
+    for k in range(2, far + 1):
+        pl.semaphore_wait(known.at[k - 2], 2)
+        if k < far:
+            tell(k)
+        send_rows(0, 0, pl.ds(0, 4), pair(k))
+    keep_rows(0, 0)
     trades = []
     for a in range(4):
         stage[1, a] = jnp.where(b_first, raw[a, 0], raw[a, 1])
         trade = remote(stage.at[1, a], xrecv.at[a], xs.at[a], xr.at[a], (partner, z))
         trade.start()
         trades.append(trade)
-    for load in loads[4:]:
+    for load in loads[4:-1]:
         load.wait()
     segs_in = seg_ref[...].astype(F32)
     seg0 = jnp.broadcast_to(segs_in[0:1, 0:1], (8, LANES))
@@ -162,7 +192,8 @@
     for a in range(4):
         trades[a].wait()
         stage[2, a] = jnp.where(stays, stage[1, a], xrecv[a])
-    send_rows(1, 2, pl.ds(0, 4))
+    send_rows(1, 2, pl.ds(0, 4), by_distance)
+    keep_rows(1, 2)
     send_ids(1, 2)
 
     q_gain, k_gain = column(qg_ref[...]), column(kg_ref[...])
@@ -252,36 +283,45 @@
         swap.start()
         swap.wait()
         total = total + gain_recv[i]
-    gain_ref[...] = total
+    gain_sum[...] = total
+    gain_out = pltpu.make_async_copy(gain_sum, gain_ref, load_sem.at[0])
+    gain_out.start()
 
     for p in range(2):
         arrived(ab_ref.at[p], outr.at[p])
         arrived(stage.at[2 * p, :, :, pl.ds(0, lanes - LANES)], zs.at[p])
         arrived(seg_all.at[p, pl.ds(0, nz - 1)], segs.at[p])
         arrived(outbuf.at[p, :, pl.ds(0, length - ROWS), :], outs.at[p])
+    gain_out.wait()
 
 
 def place_kernel(
-    moved_ref, ab_ref, gain_ref, out0, out1, out2, out3, gq_ref, gk_ref, held, in_sem, out_sem
+    moved_hbm, ab_ref, gain_hbm, out0, out1, out2, out3, gq_ref, gk_ref,
+    held, moved_ref, gain_ref, gain_low, in_sem, out_sem, small_sem,
 ):
-    dp = lax.axis_index("dp")
-    b_slot = jnp.where(moved_ref[0] == 0, 0, 1)
+    moved_in = pltpu.make_async_copy(moved_hbm, moved_ref, small_sem.at[0])
+    gain_in = pltpu.make_async_copy(gain_hbm, gain_ref, small_sem.at[1])
+    moved_in.start()
     pairs = [(a, p) for p in range(2) for a in range(4)]
-    outs = (out0, out1, out2, out3)
     loads = [
         pltpu.make_async_copy(ab_ref.at[p, a], held.at[p, a], in_sem.at[p, a]) for a, p in pairs
     ]
-    stores = [
-        pltpu.make_async_copy(
-            held.at[p, a], outs[a].at[1 - b_slot if p == 0 else b_slot], out_sem.at[p, a]
-        )
-        for a, p in pairs
-    ]
     for load in loads:
         load.start()
-    for load, store in zip(loads, stores):
+    gain_in.start()
+    moved_in.wait()
+    b_slot = jnp.where(moved_ref[0] == 0, 0, 1)
+    outs = (out0, out1, out2, out3)
+    stores = []
+    for load, (a, p) in zip(loads, pairs):
+        slot = 1 - b_slot if p == 0 else b_slot
         load.wait()
-        store.start()
+        stores.append(
+            pltpu.make_async_copy(held.at[p, a], outs[a].at[slot], out_sem.at[p, a])
+        )
+        stores[-1].start()
+    gain_in.wait()
+    dp = lax.axis_index("dp")
     lane = lax.broadcasted_iota(jnp.int32, (1, LANES), 1)
     down = lax.broadcasted_iota(jnp.int32, (2, 2), 0)
     across = lax.broadcasted_iota(jnp.int32, (2, 2), 1)
@@ -293,7 +333,9 @@
                 chosen = lane == h * HEAD_DIM + 2 * dp + j
                 value = jnp.sum(jnp.where(chosen, row, 0.0), axis=1, keepdims=True)
                 total = jnp.where((down == h) & (across == j), value, total)
-        ref[...] = total
+        gain_low[i] = total
+        stores.append(pltpu.make_async_copy(gain_low.at[i], ref, small_sem.at[2 + i]))
+        stores[-1].start()
     for store in stores:
         store.wait()
 
@@ -303,8 +345,6 @@
     block = min(256, length)
     hops = ndp.bit_length() - 1
     anywhere = pl.BlockSpec(memory_space=pl.ANY)
-    vmem = pl.BlockSpec(memory_space=pltpu.VMEM)
-    smem = pl.BlockSpec(memory_space=pltpu.SMEM)
     dma = pltpu.SemaphoreType.DMA
     ab, gains = pl.pallas_call(
         functools.partial(main_kernel, nz, ndp, block),
@@ -312,10 +352,11 @@
             jax.ShapeDtypeStruct((2, 4, ROWS, lanes), BF16),
             jax.ShapeDtypeStruct((8, LANES), F32),
         ),
-        in_specs=[smem] + [pl.BlockSpec(memory_space=pltpu.HBM)] * 7,
-        out_specs=(anywhere, vmem),
+        in_specs=[anywhere] * 8,
+        out_specs=(anywhere, anywhere),
         scratch_shapes=[
             pltpu.VMEM((4, 2, ROWS, lanes), BF16),
+            pltpu.SMEM((1,), jnp.int32),
             pltpu.VMEM((2, ROWS), jnp.int32),
             pltpu.VMEM((2, HEAD_DIM), F32),
             pltpu.VMEM((2, HEAD_DIM), F32),
@@ -344,7 +385,9 @@
             pltpu.VMEM((2, LANES, LANES), F32),
             pltpu.VMEM((hops, 8, LANES), F32),
             pltpu.VMEM((hops, 8, LANES), F32),
-            dma((7,)),
+            pltpu.VMEM((8, LANES), F32),
+            pltpu.SemaphoreType.REGULAR((max(1, nz // 2 - 1),)),
+            dma((8,)),
             dma((4,)), dma((4,)), dma(()), dma(()),
             dma((2,)), dma((2,)), dma((2,)), dma((2,)),
             dma((2,)), dma((2,)), dma((hops,)), dma((hops,)),
@@ -359,9 +402,15 @@
     return pl.pallas_call(
         place_kernel,
         out_shape=(rows, rows, rows, rows, small, small),
-        in_specs=[smem, anywhere, vmem],
-        out_specs=(anywhere,) * 4 + (vmem, vmem),
-        scratch_shapes=[pltpu.VMEM((2, 4, ROWS, lanes), BF16), dma((2, 4)), dma((2, 4))],
+        in_specs=[anywhere] * 3,
+        out_specs=(anywhere,) * 6,
+        scratch_shapes=[
+            pltpu.VMEM((2, 4, ROWS, lanes), BF16),
+            pltpu.SMEM((1,), jnp.int32),
+            pltpu.VMEM((8, LANES), F32),
+            pltpu.VMEM((2, 2, 2), F32),
+            dma((2, 4)), dma((2, 4)), dma((4,)),
+        ],
         compiler_params=pltpu.CompilerParams(vmem_limit_bytes=60 << 20),
         name="place",
     )(moved, ab, gains)

time: 205 us -> 201 us (0.980)
  the two profiles are of different devices: /device:TPU:1 before, /device:TPU:196 now
where the time goes in v3:
time: 201 us
  Pallas kernels  200 us (100%)
    pallas_call x1, Pallas kernels, body(): pl.pallas_call(functools.partial(main_kernel, nz, ndp, block), out_shape=...  197 us

profile of v3, /device:TPU:196, one launch (start us, length us, event | category | flops | bytes accessed | tf_op | source)
XLA Modules:
  0.0 200.8 jit_solution(15517142358173339858)
XLA Ops:
  1.3 197.1 %attend.1 = (bf16[2,4,64,2048]{3,2,1,0:T(8,128)(2,1)}, f32[8,128]{1,0:T(8,128)}) custom-call(s32[1]{0:T(128)S(6)} %copy.14.moved_hbm, bf16[2,64,2048]{2,1,0:T(8,128)(2,1)} %q_ref.1, bf16[2,64,2048]{2,1,0:T(8,128)(2,1)} %k_ref.1, bf16[2,64,2048]{2,1,0:T(8,128)(2,1)} %v_ref.1, bf16[2,64,2048]{2,1,0:T(8,128)(2,1)} %c_ref.1, s32[2,64]{1,0:T(2,128)} %seg_hbm.1, ...), custom_call_target="tpu_custom_call" | custom-call | tf_op jit(solution)/shard_map/attend/pallas_call | solution.py:349
  198.4 2.4 %place.1 = (bf16[2,64,2048]{2,1,0:T(8,128)(2,1)}, bf16[2,64,2048]{2,1,0:T(8,128)(2,1)}, bf16[2,64,2048]{2,1,0:T(8,128)(2,1)}, bf16[2,64,2048]{2,1,0:T(8,128)(2,1)}, f32[2,2]{1,0:T(2,128)}, /*index=5*/f32[2,2]{1,0:T(2,128)}) custom-call(s32[1]{0:T(128)S(6)} %copy.14.moved_hbm, bf16[2,4,64,2048]{3,2,1,0:T(8,128)(2,1)} %get-tuple-element.8.ab_ref, ...), custom_call_target="tpu_custom_call" | custom-call | tf_op jit(solution)/shard_map/place/pallas_call | solution.py:402

commit v4 on v3

--- a/solution.py
+++ b/solution.py
@@ -178,8 +178,8 @@
     for load in loads[4:-1]:
         load.wait()
     segs_in = seg_ref[...].astype(F32)
-    seg0 = jnp.broadcast_to(segs_in[0:1, 0:1], (8, LANES))
-    seg1 = jnp.broadcast_to(segs_in[1:2, 0:1], (8, LANES))
+    seg0 = jnp.broadcast_to(segs_in[0:1, 0:1], (1, LANES))
+    seg1 = jnp.broadcast_to(segs_in[1:2, 0:1], (1, LANES))
     seg_stage[0] = jnp.where(b_first, seg1, seg0)
     seg_stage[1] = jnp.where(b_first, seg0, seg1)
     seg_trade = remote(seg_stage.at[1], seg_x, xsegs, xsegr, (partner, z))
@@ -209,7 +209,7 @@
         def split_across(x):
             return jnp.where(left, x, 0.0).astype(BF16), jnp.where(left, 0.0, x).astype(BF16)
 
-        ids = seg_all[p, :, 0:1, :]
+        ids = seg_all[p]
         spread = jnp.broadcast_to(ids, (nz, ROWS, LANES)).reshape(length, LANES)
         seg_col[...] = spread
         seg_row[...] = jnp.transpose(spread)[0:8, :]
@@ -364,9 +364,9 @@
             pltpu.VMEM((4, ROWS, lanes), BF16),
             pltpu.VMEM((2, 4, length, LANES), BF16),
             pltpu.VMEM((2, 4, length, LANES), BF16),
-            pltpu.VMEM((3, 8, LANES), F32),
-            pltpu.VMEM((8, LANES), F32),
-            pltpu.VMEM((2, nz, 8, LANES), F32),
+            pltpu.VMEM((3, 1, LANES), F32),
+            pltpu.VMEM((1, LANES), F32),
+            pltpu.VMEM((2, nz, 1, LANES), F32),
             pltpu.VMEM((LANES, length), F32),
             pltpu.VMEM((LANES, length), F32),
             pltpu.VMEM((2, 1, length), F32),

time: 201 us -> 196 us (0.975)
  the two profiles are of different devices: /device:TPU:196 before, /device:TPU:198 now
where the time goes in v4:
time: 196 us
  Pallas kernels  195 us (99%)
    pallas_call x1, Pallas kernels, body(): pl.pallas_call(functools.partial(main_kernel, nz, ndp, block), out_shape=...  192 us

profile of v4, /device:TPU:198, one launch (start us, length us, event | category | flops | bytes accessed | tf_op | source)
XLA Modules:
  0.0 195.9 jit_solution(947711943194979691)
XLA Ops:
  1.3 192.2 %attend.1 = (bf16[2,4,64,2048]{3,2,1,0:T(8,128)(2,1)}, f32[8,128]{1,0:T(8,128)}) custom-call(s32[1]{0:T(128)S(6)} %copy.14.moved_hbm, bf16[2,64,2048]{2,1,0:T(8,128)(2,1)} %q_ref.1, bf16[2,64,2048]{2,1,0:T(8,128)(2,1)} %k_ref.1, bf16[2,64,2048]{2,1,0:T(8,128)(2,1)} %v_ref.1, bf16[2,64,2048]{2,1,0:T(8,128)(2,1)} %c_ref.1, s32[2,64]{1,0:T(2,128)} %seg_hbm.1, ...), custom_call_target="tpu_custom_call" | custom-call | tf_op jit(solution)/shard_map/attend/pallas_call | solution.py:349
  193.5 2.4 %place.1 = (bf16[2,64,2048]{2,1,0:T(8,128)(2,1)}, bf16[2,64,2048]{2,1,0:T(8,128)(2,1)}, bf16[2,64,2048]{2,1,0:T(8,128)(2,1)}, bf16[2,64,2048]{2,1,0:T(8,128)(2,1)}, f32[2,2]{1,0:T(2,128)}, /*index=5*/f32[2,2]{1,0:T(2,128)}) custom-call(s32[1]{0:T(128)S(6)} %copy.14.moved_hbm, bf16[2,4,64,2048]{3,2,1,0:T(8,128)(2,1)} %get-tuple-element.8.ab_ref, ...), custom_call_target="tpu_custom_call" | custom-call | tf_op jit(solution)/shard_map/place/pallas_call | solution.py:402

commit v5 on v4

--- a/solution.py
+++ b/solution.py
@@ -81,9 +81,6 @@
     loads = [
         pltpu.make_async_copy(src, dst, load_sem.at[i]) for i, (src, dst) in enumerate(pairs)
     ]
-    for load in [loads[-1]] + loads[:-1]:
-        load.start()
-
     by_distance = sorted(range(1, nz), key=lambda d: (-min(d, nz - d), d))
 
     bits = [1 << i for i in range(ndp.bit_length() - 1)]
@@ -92,6 +89,9 @@
     barrier = pltpu.get_barrier_semaphore()
     for peer in beside + [(g, z) for g in across]:
         pl.semaphore_signal(barrier, inc=1, device_id=peer, device_id_type=MESH)
+
+    for load in [loads[-1]] + loads[:-1]:
+        load.start()
 
     def tell(k):
         for peer in beside:
@@ -116,12 +116,11 @@
             zr.at[p],
         ).start()
 
-    def send_ids(p, slot):
-        seg_all[p, z] = seg_stage[slot]
+    def send_ids():
+        seg_all[z] = seg_stage[1]
         for d in by_distance:
             remote(
-                seg_stage.at[slot], seg_all.at[p, z], segs.at[p], segr.at[p],
-                (dp, lax.rem(z + d, nz)),
+                seg_stage.at[1], seg_all.at[z], segs, segr, (dp, lax.rem(z + d, nz))
             ).start()
 
     def send_results(p):
@@ -180,21 +179,22 @@
     segs_in = seg_ref[...].astype(F32)
     seg0 = jnp.broadcast_to(segs_in[0:1, 0:1], (1, LANES))
     seg1 = jnp.broadcast_to(segs_in[1:2, 0:1], (1, LANES))
-    seg_stage[0] = jnp.where(b_first, seg1, seg0)
-    seg_stage[1] = jnp.where(b_first, seg0, seg1)
-    seg_trade = remote(seg_stage.at[1], seg_x, xsegs, xsegr, (partner, z))
+    seg_a = jnp.where(b_first, seg1, seg0)
+    seg_b = jnp.where(b_first, seg0, seg1)
+    seg_stage[0] = seg_b
+    seg_trade = remote(seg_stage.at[0], seg_x, xsegs, xsegr, (partner, z))
     seg_trade.start()
-    send_ids(0, 0)
 
     stays = moved == 2
     seg_trade.wait()
-    seg_stage[2] = jnp.where(stays, seg_stage[1], seg_x[...])
+    half = lax.broadcasted_iota(jnp.int32, (1, LANES), 1) < HEAD_DIM
+    seg_stage[1] = jnp.where(half, seg_a, jnp.where(stays, seg_b, seg_x[...]))
+    send_ids()
     for a in range(4):
         trades[a].wait()
         stage[2, a] = jnp.where(stays, stage[1, a], xrecv[a])
     send_rows(1, 2, pl.ds(0, 4), by_distance)
     keep_rows(1, 2)
-    send_ids(1, 2)
 
     q_gain, k_gain = column(qg_ref[...]), column(kg_ref[...])
     gain_acc[...] = jnp.zeros_like(gain_acc)
@@ -209,7 +209,7 @@
         def split_across(x):
             return jnp.where(left, x, 0.0).astype(BF16), jnp.where(left, 0.0, x).astype(BF16)
 
-        ids = seg_all[p]
+        ids = seg_all[:, :, p * HEAD_DIM : p * HEAD_DIM + 1]
         spread = jnp.broadcast_to(ids, (nz, ROWS, LANES)).reshape(length, LANES)
         seg_col[...] = spread
         seg_row[...] = jnp.transpose(spread)[0:8, :]
@@ -270,7 +270,8 @@
 
     for p in range(2):
         arrived(inbuf.at[p], zr.at[p])
-        arrived(seg_all.at[p, pl.ds(0, nz - 1)], segr.at[p])
+        if p == 0:
+            arrived(seg_all.at[pl.ds(0, nz - 1)], segr)
         compute(p)
         send_results(p)
 
@@ -290,8 +291,8 @@
     for p in range(2):
         arrived(ab_ref.at[p], outr.at[p])
         arrived(stage.at[2 * p, :, :, pl.ds(0, lanes - LANES)], zs.at[p])
-        arrived(seg_all.at[p, pl.ds(0, nz - 1)], segs.at[p])
         arrived(outbuf.at[p, :, pl.ds(0, length - ROWS), :], outs.at[p])
+    arrived(seg_all.at[pl.ds(0, nz - 1)], segs)
     gain_out.wait()
 
 
@@ -364,9 +365,9 @@
             pltpu.VMEM((4, ROWS, lanes), BF16),
             pltpu.VMEM((2, 4, length, LANES), BF16),
             pltpu.VMEM((2, 4, length, LANES), BF16),
-            pltpu.VMEM((3, 1, LANES), F32),
+            pltpu.VMEM((2, 1, LANES), F32),
             pltpu.VMEM((1, LANES), F32),
-            pltpu.VMEM((2, nz, 1, LANES), F32),
+            pltpu.VMEM((nz, 1, LANES), F32),
             pltpu.VMEM((LANES, length), F32),
             pltpu.VMEM((LANES, length), F32),
             pltpu.VMEM((2, 1, length), F32),
@@ -389,7 +390,7 @@
             pltpu.SemaphoreType.REGULAR((max(1, nz // 2 - 1),)),
             dma((8,)),
             dma((4,)), dma((4,)), dma(()), dma(()),
-            dma((2,)), dma((2,)), dma((2,)), dma((2,)),
+            dma((2,)), dma((2,)), dma(()), dma(()),
             dma((2,)), dma((2,)), dma((hops,)), dma((hops,)),
         ],
         compiler_params=pltpu.CompilerParams(

time: 196 us -> 196 us (level)
  the two profiles are of different devices: /device:TPU:198 before, /device:TPU:195 now
where the time goes in v5:
time: 196 us
  Pallas kernels  194 us (99%)
    pallas_call x1, Pallas kernels, body(): pl.pallas_call(functools.partial(main_kernel, nz, ndp, block), out_shape=...  192 us

profile of v5, /device:TPU:195, one launch (start us, length us, event | category | flops | bytes accessed | tf_op | source)
XLA Modules:
  0.0 195.6 jit_solution(15346119223913125113)
XLA Ops:
  1.3 191.9 %attend.1 = (bf16[2,4,64,2048]{3,2,1,0:T(8,128)(2,1)}, f32[8,128]{1,0:T(8,128)}) custom-call(s32[1]{0:T(128)S(6)} %copy.14.moved_hbm, bf16[2,64,2048]{2,1,0:T(8,128)(2,1)} %q_ref.1, bf16[2,64,2048]{2,1,0:T(8,128)(2,1)} %k_ref.1, bf16[2,64,2048]{2,1,0:T(8,128)(2,1)} %v_ref.1, bf16[2,64,2048]{2,1,0:T(8,128)(2,1)} %c_ref.1, s32[2,64]{1,0:T(2,128)} %seg_hbm.1, ...), custom_call_target="tpu_custom_call" | custom-call | tf_op jit(solution)/shard_map/attend/pallas_call | solution.py:350
  193.2 2.4 %place.1 = (bf16[2,64,2048]{2,1,0:T(8,128)(2,1)}, bf16[2,64,2048]{2,1,0:T(8,128)(2,1)}, bf16[2,64,2048]{2,1,0:T(8,128)(2,1)}, bf16[2,64,2048]{2,1,0:T(8,128)(2,1)}, f32[2,2]{1,0:T(2,128)}, /*index=5*/f32[2,2]{1,0:T(2,128)}) custom-call(s32[1]{0:T(128)S(6)} %copy.14.moved_hbm, bf16[2,4,64,2048]{3,2,1,0:T(8,128)(2,1)} %get-tuple-element.8.ab_ref, ...), custom_call_target="tpu_custom_call" | custom-call | tf_op jit(solution)/shard_map/place/pallas_call | solution.py:403
